TPU v7x, 32 devices: a whole 2x2x4 slice. The times are simulated.
32 devices in a mesh: fsdp: 8 (over z, y), ctx: 2 (over x), tp: 2 (over core).
Axes of the slice: x: 2, y: 2, z: 4, core: 2. Of those that a mesh axis runs over, the one named last changes fastest.
Arguments:
- tokens: bfloat16 [2, 8192, 768], P(None, ('fsdp', 'ctx')), may hold values from -6 to 6
- gain_attn: bfloat16 [768], P('fsdp'), may hold values from 0.099609375 to 1.8984375
- w_query: bfloat16 [768, 768], P('fsdp', 'tp'), may hold values from -0.21875 to 0.21875
- w_key: bfloat16 [768, 768], P('fsdp', 'tp'), may hold values from -0.21875 to 0.21875
- w_value: bfloat16 [768, 768], P('fsdp', 'tp'), may hold values from -0.21875 to 0.21875
- w_out: bfloat16 [768, 768], P('tp', 'fsdp'), may hold values from -6 to 6
- gain_ffn: bfloat16 [768], P('fsdp'), may hold values from 0.099609375 to 1.8984375
- w_gate: bfloat16 [768, 1152], P('fsdp', 'tp'), may hold values from -0.21875 to 0.21875
- w_up: bfloat16 [768, 1152], P('fsdp', 'tp'), may hold values from -0.21875 to 0.21875
- w_down: bfloat16 [1152, 768], P('tp', 'fsdp'), may hold values from -0.1875 to 0.1875
- cotangent: bfloat16 [2, 8192, 768], P(None, ('fsdp', 'ctx')), may hold values from -6 to 6
Outputs:
- output: bfloat16 [2, 8192, 768], P(None, ('fsdp', 'ctx'))
- grad_tokens: float32 [2, 8192, 768], P(None, ('fsdp', 'ctx'))
- grad_gain_attn: float32 [768], P('fsdp')
- grad_query: float32 [768, 768], P('fsdp', 'tp')
- grad_key: float32 [768, 768], P('fsdp', 'tp')
- grad_value: float32 [768, 768], P('fsdp', 'tp')
- grad_out: float32 [768, 768], P('tp', 'fsdp')
- grad_gain_ffn: float32 [768], P('fsdp')
- grad_gate: float32 [768, 1152], P('fsdp', 'tp')
- grad_up: float32 [768, 1152], P('fsdp', 'tp')
- grad_down: float32 [1152, 768], P('tp', 'fsdp')
All inputs are finite; a program needn't handle non-finite values.
Results may differ from a plain program's by a relative error of at most 0.025.
Values may be sent and summed in bfloat16 or wider, within the bound.
A program may use at most 192 MiB of HBM per device.

v0:
```python
from functools import partial

import jax
import jax.numpy as jnp
from jax import lax
from jax.sharding import PartitionSpec as P

HD = 64


eps_norm = 1e-05
rope_base = 160000.0


def layer_norm(x):
    mean = jnp.mean(x, axis=-1, keepdims=True)
    centred = x - mean
    var = jnp.mean(centred * centred, axis=-1, keepdims=True)
    rstd = lax.rsqrt(var + eps_norm)
    return (centred * rstd, rstd)


def norm_back(grad_normed, normed, rstd):
    first = jnp.mean(grad_normed, axis=-1, keepdims=True)
    second = jnp.mean(grad_normed * normed, axis=-1, keepdims=True)
    return rstd * (grad_normed - first - normed * second)


def rope_angles(first, count, width):
    position = (first + jnp.arange(count, dtype=jnp.int32)).astype(jnp.float32)
    inverse = 1.0 / rope_base ** (
        jnp.arange(0, width, 2, dtype=jnp.int32).astype(jnp.float32) / width
    )
    angle = position[:, None] * inverse[None, :]
    angle = jnp.concatenate([angle, angle], axis=-1)
    return (jnp.cos(angle), jnp.sin(angle))


def rotate(heads, cosine, sine, sign):
    half = heads.shape[-1] // 2
    turned = jnp.concatenate([-heads[..., half:], heads[..., :half]], axis=-1)
    return heads * cosine[:, None, :] + sign * turned * sine[:, None, :]


def matmul(a, b):
    return jnp.dot(a, b, preferred_element_type=jnp.float32)


def on_device(
    tokens, gain_attn, w_query, w_key, w_value, w_out, gain_ffn, w_gate, w_up, w_down, cotangent
):
    full = (
        lax.all_gather(gain_attn, "fsdp", axis=0, tiled=True),
        lax.all_gather(w_query, "fsdp", axis=0, tiled=True),
        lax.all_gather(w_key, "fsdp", axis=0, tiled=True),
        lax.all_gather(w_value, "fsdp", axis=0, tiled=True),
        lax.all_gather(w_out, "fsdp", axis=1, tiled=True),
        lax.all_gather(gain_ffn, "fsdp", axis=0, tiled=True),
        lax.all_gather(w_gate, "fsdp", axis=0, tiled=True),
        lax.all_gather(w_up, "fsdp", axis=0, tiled=True),
        lax.all_gather(w_down, "fsdp", axis=1, tiled=True),
    )
    gain_one = full[0].astype(jnp.float32)
    gain_two = full[5].astype(jnp.float32)
    slots = tokens.shape[0]
    rows = tokens.shape[1]
    model = tokens.shape[2]
    flat = slots * rows
    x = tokens.astype(jnp.float32).reshape(flat, model)
    width = full[1].shape[1]
    heads = width // HD
    scale = HD ** (-0.5)
    cosine, sine = rope_angles(lax.axis_index("ctx") * rows, rows, HD)
    normed_one, rstd_one = layer_norm(x)
    h_one = (normed_one * gain_one).astype(jnp.bfloat16)
    query = rotate(
        matmul(h_one, full[1]).reshape(slots, rows, heads, HD), cosine, sine, 1.0
    ).astype(jnp.bfloat16)
    key_flat = (
        rotate(matmul(h_one, full[2]).reshape(slots, rows, heads, HD), cosine, sine, 1.0)
        .astype(jnp.bfloat16)
        .reshape(slots, rows, width)
    )
    value_flat = matmul(h_one, full[3]).astype(jnp.bfloat16).reshape(slots, rows, width)
    piece = (
        lax.all_gather(key_flat, "ctx", axis=1, tiled=True),
        lax.all_gather(value_flat, "ctx", axis=1, tiled=True),
    )
    best = jnp.full((slots, heads, rows), -1e30, jnp.float32)
    keys = piece[0].reshape(slots, -1, heads, HD)
    values = piece[1].reshape(slots, -1, heads, HD)
    scores = jnp.einsum("bqhd,bkhd->bhqk", query, keys, preferred_element_type=jnp.float32) * scale
    newbest = jnp.maximum(best, jnp.max(scores, axis=-1))
    weights = jnp.exp(scores - newbest[..., None])
    total = jnp.sum(weights, axis=-1)
    accum = jnp.einsum(
        "bhqk,bkhd->bhqd", weights.astype(jnp.bfloat16), values, preferred_element_type=jnp.float32
    )
    best, total, accum = (newbest, total, accum)
    log_total = best + jnp.log(total)
    attended = (
        (accum / total[..., None]).transpose(0, 2, 1, 3).reshape(flat, width).astype(jnp.bfloat16)
    )
    x_two = x + lax.psum(matmul(attended, full[4]).astype(jnp.bfloat16), "tp").astype(jnp.float32)
    normed_two, rstd_two = layer_norm(x_two)
    h_two = (normed_two * gain_two).astype(jnp.bfloat16)
    gate = matmul(h_two, full[6])
    up_part = matmul(h_two, full[7])
    activated, gelu_back = jax.vjp(partial(jax.nn.gelu, approximate=False), gate)
    hidden = (activated * up_part).astype(jnp.bfloat16)
    result = x_two + lax.psum(matmul(hidden, full[8]).astype(jnp.bfloat16), "tp").astype(
        jnp.float32
    )
    output = result.astype(jnp.bfloat16).reshape(slots, rows, model)
    grad_y = cotangent.astype(jnp.float32).reshape(flat, model)
    grad_low = grad_y.astype(jnp.bfloat16)
    grad_hidden = matmul(grad_low, full[8].T)
    grad_down = matmul(hidden.T, grad_low)
    grad_gate_act = gelu_back(grad_hidden * up_part)[0].astype(jnp.bfloat16)
    grad_up_act = (grad_hidden * activated).astype(jnp.bfloat16)
    grad_gate = matmul(h_two.T, grad_gate_act)
    grad_up = matmul(h_two.T, grad_up_act)
    grad_h_two = lax.psum(
        (matmul(grad_gate_act, full[6].T) + matmul(grad_up_act, full[7].T)).astype(jnp.bfloat16),
        "tp",
    ).astype(jnp.float32)
    grad_gain_ffn = jnp.sum(grad_h_two * normed_two, axis=0)
    grad_x_two = grad_y + norm_back(grad_h_two * gain_two, normed_two, rstd_two)
    branch_low = grad_x_two.astype(jnp.bfloat16)
    grad_out = matmul(attended.T, branch_low)
    grad_att = matmul(branch_low, full[4].T).astype(jnp.bfloat16)
    delta_rows = jnp.sum(
        (grad_att.astype(jnp.float32) * attended.astype(jnp.float32)).reshape(
            slots, rows, heads, HD
        ),
        axis=-1,
    )
    delta = delta_rows.transpose(0, 2, 1)
    grad_att_heads = grad_att.reshape(slots, rows, heads, HD)
    stats_all = (
        lax.all_gather(log_total.transpose(0, 2, 1), "ctx", axis=1, tiled=True),
        lax.all_gather(delta_rows, "ctx", axis=1, tiled=True),
    )
    own_keys = key_flat.reshape(slots, rows, heads, HD)
    own_values = value_flat.reshape(slots, rows, heads, HD)
    piece = (
        lax.all_gather(query, "ctx", axis=1, tiled=True),
        lax.all_gather(grad_att_heads, "ctx", axis=1, tiled=True),
    )
    queries = piece[0]
    grads_in = piece[1]
    lse_piece = stats_all[0].transpose(0, 2, 1)
    delta_piece = stats_all[1].transpose(0, 2, 1)
    scores = (
        jnp.einsum("bqhd,bkhd->bhqk", queries, own_keys, preferred_element_type=jnp.float32) * scale
    )
    probs = jnp.exp(scores - lse_piece[..., None])
    grad_probs = jnp.einsum(
        "bqhd,bkhd->bhqk", grads_in, own_values, preferred_element_type=jnp.float32
    )
    grad_scores = (probs * (grad_probs - delta_piece[..., None])).astype(jnp.bfloat16)
    grad_keys_acc = (
        jnp.einsum("bhqk,bqhd->bkhd", grad_scores, queries, preferred_element_type=jnp.float32)
        * scale
    )
    grad_values_acc = jnp.einsum(
        "bhqk,bqhd->bkhd", probs.astype(jnp.bfloat16), grads_in, preferred_element_type=jnp.float32
    )
    piece = (
        lax.all_gather(key_flat, "ctx", axis=1, tiled=True),
        lax.all_gather(value_flat, "ctx", axis=1, tiled=True),
    )
    keys = piece[0].reshape(slots, -1, heads, HD)
    values = piece[1].reshape(slots, -1, heads, HD)
    scores = jnp.einsum("bqhd,bkhd->bhqk", query, keys, preferred_element_type=jnp.float32) * scale
    probs = jnp.exp(scores - log_total[..., None])
    grad_probs = jnp.einsum(
        "bqhd,bkhd->bhqk", grad_att_heads, values, preferred_element_type=jnp.float32
    )
    grad_scores = (probs * (grad_probs - delta[..., None])).astype(jnp.bfloat16)
    probs, grad_scores = (probs, grad_scores)
    grad_query_rot = (
        jnp.einsum("bhqk,bkhd->bqhd", grad_scores, keys, preferred_element_type=jnp.float32) * scale
    )
    grad_query_raw = (
        rotate(grad_query_rot, cosine, sine, -1.0).reshape(flat, width).astype(jnp.bfloat16)
    )
    grad_key_raw = (
        rotate(grad_keys_acc, cosine, sine, -1.0).reshape(flat, width).astype(jnp.bfloat16)
    )
    grad_value_raw = grad_values_acc.reshape(flat, width).astype(jnp.bfloat16)
    grad_query = matmul(h_one.T, grad_query_raw)
    grad_key = matmul(h_one.T, grad_key_raw)
    grad_value = matmul(h_one.T, grad_value_raw)
    grad_h_one = lax.psum(
        (
            matmul(grad_query_raw, full[1].T)
            + matmul(grad_key_raw, full[2].T)
            + matmul(grad_value_raw, full[3].T)
        ).astype(jnp.bfloat16),
        "tp",
    ).astype(jnp.float32)
    grad_gain_attn = jnp.sum(grad_h_one * normed_one, axis=0)
    grad_tokens = (grad_x_two + norm_back(grad_h_one * gain_one, normed_one, rstd_one)).reshape(
        slots, rows, model
    )
    pieces = (
        lax.psum_scatter(
            grad_gain_attn.astype(jnp.bfloat16), "fsdp", scatter_dimension=0, tiled=True
        ).astype(jnp.float32),
        lax.psum_scatter(
            grad_query.astype(jnp.bfloat16), "fsdp", scatter_dimension=0, tiled=True
        ).astype(jnp.float32),
        lax.psum_scatter(
            grad_key.astype(jnp.bfloat16), "fsdp", scatter_dimension=0, tiled=True
        ).astype(jnp.float32),
        lax.psum_scatter(
            grad_value.astype(jnp.bfloat16), "fsdp", scatter_dimension=0, tiled=True
        ).astype(jnp.float32),
        lax.psum_scatter(
            grad_out.astype(jnp.bfloat16), "fsdp", scatter_dimension=1, tiled=True
        ).astype(jnp.float32),
        lax.psum_scatter(
            grad_gain_ffn.astype(jnp.bfloat16), "fsdp", scatter_dimension=0, tiled=True
        ).astype(jnp.float32),
        lax.psum_scatter(
            grad_gate.astype(jnp.bfloat16), "fsdp", scatter_dimension=0, tiled=True
        ).astype(jnp.float32),
        lax.psum_scatter(
            grad_up.astype(jnp.bfloat16), "fsdp", scatter_dimension=0, tiled=True
        ).astype(jnp.float32),
        lax.psum_scatter(
            grad_down.astype(jnp.bfloat16), "fsdp", scatter_dimension=1, tiled=True
        ).astype(jnp.float32),
    )
    owned = (
        lax.psum(pieces[0].astype(jnp.bfloat16), "ctx").astype(jnp.float32),
        lax.psum(pieces[1].astype(jnp.bfloat16), "ctx").astype(jnp.float32),
        lax.psum(pieces[2].astype(jnp.bfloat16), "ctx").astype(jnp.float32),
        lax.psum(pieces[3].astype(jnp.bfloat16), "ctx").astype(jnp.float32),
        lax.psum(pieces[4].astype(jnp.bfloat16), "ctx").astype(jnp.float32),
        lax.psum(pieces[5].astype(jnp.bfloat16), "ctx").astype(jnp.float32),
        lax.psum(pieces[6].astype(jnp.bfloat16), "ctx").astype(jnp.float32),
        lax.psum(pieces[7].astype(jnp.bfloat16), "ctx").astype(jnp.float32),
        lax.psum(pieces[8].astype(jnp.bfloat16), "ctx").astype(jnp.float32),
    )
    return (
        output,
        grad_tokens,
        owned[0],
        owned[1],
        owned[2],
        owned[3],
        owned[4],
        owned[5],
        owned[6],
        owned[7],
        owned[8],
    )


def solution(mesh):
    placed = (
        P(None, ("fsdp", "ctx"), None),
        P("fsdp"),
        P("fsdp", "tp"),
        P("fsdp", "tp"),
        P("fsdp", "tp"),
        P("tp", "fsdp"),
        P("fsdp"),
        P("fsdp", "tp"),
        P("fsdp", "tp"),
        P("tp", "fsdp"),
        P(None, ("fsdp", "ctx"), None),
    )
    return jax.shard_map(
        on_device,
        mesh=mesh,
        in_specs=placed,
        out_specs=(
            P(None, ("fsdp", "ctx"), None),
            P(None, ("fsdp", "ctx"), None),
            P("fsdp"),
            P("fsdp", "tp"),
            P("fsdp", "tp"),
            P("fsdp", "tp"),
            P("tp", "fsdp"),
            P("fsdp"),
            P("fsdp", "tp"),
            P("fsdp", "tp"),
            P("tp", "fsdp"),
        ),
        check_vma=False,
    )
```

profile of v0, /device:TPU:0, one launch (start us, length us, event | category | flops | bytes accessed | tf_op | source)
XLA Modules:
  0.0 980.2 jit_solution(7829995417398144050)
XLA Ops:
  11.0 23.1 %all-reduce.5 = (bf16[768]{0:T(1024)(128)(2,1)S(1)}, bf16[768]{0:T(1024)(128)(2,1)S(1)}) all-reduce(bf16[768]{0:T(1024)(128)(2,1)S(1)} %dynamic-update-slice.1, bf16[768]{0:T(1024)(128)(2,1)S(1)} %dynamic-update-slice), channel_id=1, replica_groups=mesh['fsdp'=8,'ctx'=2,'tp'=2] {'fsdp'}, use_global_device_ids=true, to_apply=%add.1 | all-reduce | flops 1536 | bytes 6144
  36.5 31.9 %all_gather.49 = bf16[768,384]{1,0:T(8,128)(2,1)S(1)} all-gather(bf16[96,384]{1,0:T(8,128)(2,1)S(1)} %copy-done.43), channel_id=1, replica_groups=mesh['fsdp'=8,'ctx'=2,'tp'=2] {'fsdp'}, dimensions={0}, use_global_device_ids=true | all-gather | bytes 663552 | tf_op jit(solution)/shard_map/all_gather | solution.py:55
  70.3 31.6 %all_gather.48 = bf16[768,384]{1,0:T(8,128)(2,1)S(1)} all-gather(bf16[96,384]{1,0:T(8,128)(2,1)S(1)} %copy-done.44), channel_id=1, replica_groups=mesh['fsdp'=8,'ctx'=2,'tp'=2] {'fsdp'}, dimensions={0}, use_global_device_ids=true | all-gather | bytes 663552 | tf_op jit(solution)/shard_map/all_gather | solution.py:54
  105.1 2.0 fusion.56
  107.4 1.9 slice_negate_fusion.2
  109.3 3.2 fusion.48
  112.6 31.5 %all_gather.51 = bf16[768,384]{1,0:T(8,128)(2,1)S(1)} all-gather(bf16[96,384]{1,0:T(8,128)(2,1)S(1)} %copy-done.45), channel_id=1, replica_groups=mesh['fsdp'=8,'ctx'=2,'tp'=2] {'fsdp'}, dimensions={0}, use_global_device_ids=true | all-gather | bytes 663552 | tf_op jit(solution)/shard_map/all_gather | solution.py:56
  144.7 1.9 convolution_convert_fusion.6
  146.7 33.5 %all_gather.53 = bf16[384,768]{0,1:T(8,128)(2,1)} all-gather(bf16[384,96]{0,1:T(8,128)(2,1)S(1)} %copy-done.46), channel_id=1, replica_groups=mesh['fsdp'=8,'ctx'=2,'tp'=2] {'fsdp'}, dimensions={1}, use_global_device_ids=true | all-gather | bytes 663552 | tf_op jit(solution)/shard_map/all_gather | solution.py:57
  180.2 11.6 %multiply_reduce_fusion = (f32[2,6,512]{2,1,0:T(8,128)S(1)}, f32[2,6,512,1024]{3,2,1,0:T(8,128)}) fusion(bf16[2,512,6,64]{1,3,2,0:T(8,128)(2,1)S(1)} %get-tuple-element.49, bf16[2,1024,6,64]{1,3,2,0:T(8,128)(2,1)} %bitcast.188), kind=kOutput, calls=%fused_computation.7 | convolution fusion | flops 817883136 | bytes 27549696 | tf_op jit(solution)/shard_map/bqhd,bkhd->bhqk/dot_general | solution.py:92
  191.8 10.9 %fusion = f32[2,6,512]{2,1,0:T(8,128)S(1)} fusion(f32[2,6,512,1024]{3,2,1,0:T(8,128)} %get-tuple-element.61, f32[2,6,512]{2,1,0:T(8,128)S(1)} %broadcast_maximum_fusion), kind=kLoop, calls=%fused_computation.4 | loop fusion | flops 18868224 | bytes 25214976 | tf_op jit(solution)/shard_map/reduce_sum | solution.py:95
  205.6 10.5 %fusion.53 = bf16[2,512,6,64]{1,3,2,0:T(8,128)(2,1)S(1)} fusion(bf16[2,1024,6,64]{1,3,2,0:T(8,128)(2,1)S(1)} %bitcast.184, f32[2,6,512,1024]{3,2,1,0:T(8,128)} %get-tuple-element.61, f32[2,6,512]{2,1,0:T(8,128)S(1)} %broadcast_maximum_fusion, f32[2,512,6]{1,2,0:T(8,128)S(1)} %bitcast.192), kind=kOutput, calls=%fused_computation.92 | convolution fusion | flops 824967168 | bytes 27574272 | tf_op jit(solution)/shard_map/bhqk,bkhd->bhqd/dot_general | solution.py:96
  217.2 2.2 convolution_convert_fusion.1
  219.5 34.8 %all_gather.55 = bf16[768,576]{1,0:T(8,128)(2,1)} all-gather(bf16[96,576]{1,0:T(8,128)(2,1)S(1)} %copy-done.40), channel_id=1, replica_groups=mesh['fsdp'=8,'ctx'=2,'tp'=2] {'fsdp'}, dimensions={0}, use_global_device_ids=true | all-gather | bytes 995328 | tf_op jit(solution)/shard_map/all_gather | solution.py:59
  254.3 35.2 %all_gather.57 = bf16[576,768]{0,1:T(8,128)(2,1)} all-gather(bf16[576,96]{0,1:T(8,128)(2,1)S(1)} %copy-done.41), channel_id=1, replica_groups=mesh['fsdp'=8,'ctx'=2,'tp'=2] {'fsdp'}, dimensions={1}, use_global_device_ids=true | all-gather | bytes 995328 | tf_op jit(solution)/shard_map/all_gather | solution.py:61
  289.5 34.2 %all_gather.56 = bf16[768,576]{1,0:T(8,128)(2,1)} all-gather(bf16[96,576]{1,0:T(8,128)(2,1)S(1)} %copy-done.42), channel_id=1, replica_groups=mesh['fsdp'=8,'ctx'=2,'tp'=2] {'fsdp'}, dimensions={0}, use_global_device_ids=true | all-gather | bytes 995328 | tf_op jit(solution)/shard_map/all_gather | solution.py:60
  323.7 2.0 fusion.38
  329.9 6.2 multiply_convert_fusion.5
  336.2 3.2 add_convert_fusion.3
  340.8 2.6 add_convert_fusion.1
  344.6 2.3 copy.44
  346.9 14.4 %all-reduce.16.cloned.1.call-done = bf16[1024,768]{1,0:T(8,128)(2,1)} async-done(((bf16[1024,768]{1,0:T(8,128)(2,1)}), bf16[1024,768]{1,0:T(8,128)(2,1)}) %all-reduce.16.cloned.1.call-update) | async-done | bytes 1572880 | tf_op jit(solution)/shard_map/psum | solution.py:123
  361.3 3.3 fusion.23
  366.4 2.4 convert_multiply_fusion.4
  368.8 2.4 copy.42
  371.2 3.3 reshape.296
  374.4 2.1 copy.43
  376.7 4.1 convolution_convert_fusion.4
  380.9 2.3 copy.49
  383.2 3.3 reshape_reshape.3
  386.4 4.2 convolution_convert_fusion.3
  390.7 4.8 all_gather.59
  396.1 13.5 %fusion.89 = f32[2,6,1024,512]{3,2,1,0:T(8,128)} fusion(bf16[2,1024,6,64]{1,3,2,0:T(8,128)(2,1)} %all-gather.9.cloned.1.call-done, bf16[2,512,6,64]{1,3,2,0:T(8,128)(2,1)} %get-tuple-element.48), kind=kOutput, calls=%fused_computation.146 | convolution fusion | flops 805306368 | bytes 27525120 | tf_op jit(solution)/shard_map/bqhd,bkhd->bhqk/dot_general | solution.py:155
  409.6 2.5 convolution_convert_fusion.2
  412.1 3.0 copy.45
  415.2 3.4 reshape.297
  418.6 1.8 reduce_sum.115
  420.4 4.7 all_gather.61
  425.8 15.9 %bitcast_multiply_fusion.2 = (f32[2,512,6,64]{1,3,2,0:T(8,128)}, f32[2,6,64,512]{3,2,1,0:T(8,128)}) fusion(bf16[2,1024,6,64]{1,3,2,0:T(8,128)(2,1)} %bitcast.189, f32[2,6,512,1024]{3,2,1,0:T(8,128)} %get-tuple-element.61, f32[2,6,512]{2,1,0:T(8,128)} %copy.46, f32[2,6,512]{2,1,0:T(8,128)} %log_add_fusion, bf16[2,1024,6,64]{1,3,2,0:T(8,128)(2,1)} %bitcast.185, ...), kind=kOutput, calls=%fused_computation.89 | convolution fusion | flops 1642463232 | bytes 32292864 | tf_op jit(solution)/shard_map/bhqk,bkhd->bqhd/dot_general | solution.py:183
  441.7 2.9 slice_negate_fusion.1
  444.6 3.0 convolution_convert_fusion.7
  447.7 11.2 %fusion.63 = bf16[2,512,6,64]{1,3,2,0:T(8,128)(2,1)S(1)} fusion(bf16[2,1024,6,64]{1,3,2,0:T(8,128)(2,1)} %all-gather.11.cloned.1.call-done, f32[2,6,1024,512]{3,2,1,0:T(8,128)} %fusion.89, f32[2,6,1024]{2,1,0:T(8,128)S(1)} %bitcast.193), kind=kOutput, calls=%fused_computation.108 | convolution fusion | flops 824573952 | bytes 27574272 | tf_op jit(solution)/shard_map/bhqk,bqhd->bkhd/dot_general | solution.py:166
  460.8 1.9 convolution_convert_fusion.8
  463.0 14.8 %bitcast_multiply_fusion = (f32[2,512,6,64]{1,3,2,0:T(8,128)}, f32[2,6,64,512]{3,2,1,0:T(8,128)}) fusion(bf16[2,1024,6,64]{1,3,2,0:T(8,128)(2,1)} %all-gather.9.cloned.1.call-done, f32[2,6,1024,512]{3,2,1,0:T(8,128)} %fusion.89, f32[2,6,1024]{2,1,0:T(8,128)S(1)} %copy.51, f32[2,6,1024]{2,1,0:T(8,128)S(1)} %bitcast.194, ...), kind=kOutput, calls=%fused_computation.87 | convolution fusion | flops 1642463232 | bytes 32342016 | tf_op jit(solution)/shard_map/bhqk,bqhd->bkhd/dot_general | solution.py:163
  480.2 3.2 fusion.52
  485.2 1.9 convolution_convert_fusion.9
  487.2 2.1 copy.47
  490.3 1.9 convolution_convert_fusion.10
  492.2 4.3 convolution_convert_fusion
  496.5 2.6 fusion.90
  499.1 53.5 %reduce-scatter.18.cloned.1.call-done = bf16[96,576]{1,0:T(8,128)(2,1)} async-done(((bf16[768,576]{1,0:T(8,128)(2,1)}), bf16[96,576]{1,0:T(8,128)(2,1)}) %reduce-scatter.18.cloned.1.call-update) | async-done | bytes 110608 | tf_op jit(solution)/shard_map/reduce_scatter | solution.py:229
  552.6 65.8 %reduce-scatter.20.cloned.1.call-done = bf16[576,96]{0,1:T(8,128)(2,1)} async-done(((bf16[576,768]{0,1:T(8,128)(2,1)}), bf16[576,96]{0,1:T(8,128)(2,1)}) %reduce-scatter.20.cloned.1.call-update) | async-done | bytes 110608 | tf_op jit(solution)/shard_map/reduce_scatter | solution.py:232
  618.4 64.7 %reduce-scatter.14.cloned.1.call-done = bf16[384,96]{0,1:T(8,128)(2,1)} async-done(((bf16[384,768]{0,1:T(8,128)(2,1)}), bf16[384,96]{0,1:T(8,128)(2,1)}) %reduce-scatter.14.cloned.1.call-update) | async-done | bytes 73744 | tf_op jit(solution)/shard_map/reduce_scatter | solution.py:220
  683.0 64.5 %reduce-scatter.12.cloned.1.call-done = bf16[96,384]{1,0:T(8,128)(2,1)} async-done(((bf16[768,384]{1,0:T(8,128)(2,1)}), bf16[96,384]{1,0:T(8,128)(2,1)}) %reduce-scatter.12.cloned.1.call-update) | async-done | bytes 73744 | tf_op jit(solution)/shard_map/reduce_scatter | solution.py:217
  747.5 64.7 %reduce-scatter.10.cloned.1.call-done = bf16[96,384]{1,0:T(8,128)(2,1)} async-done(((bf16[768,384]{1,0:T(8,128)(2,1)}), bf16[96,384]{1,0:T(8,128)(2,1)}) %reduce-scatter.10.cloned.1.call-update) | async-done | bytes 73744 | tf_op jit(solution)/shard_map/reduce_scatter | solution.py:214
  812.2 64.5 %reduce-scatter.8.cloned.1.call-done = bf16[96,384]{1,0:T(8,128)(2,1)} async-done(((bf16[768,384]{1,0:T(8,128)(2,1)}), bf16[96,384]{1,0:T(8,128)(2,1)}) %reduce-scatter.8.cloned.1.call-update) | async-done | bytes 73744 | tf_op jit(solution)/shard_map/reduce_scatter | solution.py:211
  877.0 2.5 fusion.88
  879.7 2.2 add_convert_fusion
  882.5 28.7 %all-reduce.20.cloned.1.call-done = (bf16[96,384]{1,0:T(8,128)(2,1)}, bf16[96,384]{1,0:T(8,128)(2,1)}, bf16[96,384]{1,0:T(8,128)(2,1)}, bf16[384,96]{0,1:T(8,128...) async-done(((bf16[96,384]{1,0:T(8,128)(2,1)}, bf16[96,384]{1,0:T(8,128)(2,1)}, bf16[96,384]{1,0:T(8,128)(2,1)}, ...) | async-done | bytes 626704 | tf_op jit(solution)/shard_map/psum | solution.py:238
  922.3 15.2 %all-reduce.18.cloned.1.call-done = (bf16[1024,768]{1,0:T(8,128)(2,1)}, bf16[1024,768]{1,0:T(8,128)(2,1)}) async-done(((bf16[1024,768]{1,0:T(8,128)(2,1)}, bf16[1024,768]{1,0:T(8,128)(2,1)}), (bf16[1024,768]{1,0:T(8,128)(2,1)}, bf16[1024,768]{1,0:T(8,128)(2,1)})) %all-reduce.18.cloned.1.call-update) | async-done | bytes 3145744 | tf_op jit(solution)/shard_map/psum | solution.py:111
  937.5 3.0 fusion.28
  940.5 21.6 %all-reduce.4 = (bf16[768]{0:T(1024)(128)(2,1)S(1)}, bf16[768]{0:T(1024)(128)(2,1)S(1)}) all-reduce(bf16[768]{0:T(1024)(128)(2,1)S(1)} %get-tuple-element.13, bf16[768]{0:T(1024)(128)(2,1)S(1)} %get-tuple-element.11), channel_id=2, replica_groups=mesh['fsdp'=8,'ctx'=2,'tp'=2] {'fsdp'}, use_global_device_ids=true, to_apply=%region_16.0.clone | all-reduce | flops 1536 | bytes 6144
  962.3 4.9 all-reduce.7
  968.3 5.0 fusion.26
  (194 shorter events, 45.8 us)
Async XLA Ops:
  7.2 28.7 %copy-start = (bf16[2,512,768]{2,1,0:T(8,128)(2,1)S(1)}, bf16[2,512,768]{2,1,0:T(8,128)(2,1)}, u32[]{:S(2)}) copy-start(bf16[2,512,768]{2,1,0:T(8,128)(2,1)} %param.11) | copy-start | bytes 4718596
  7.2 29.3 %copy-start.43 = (bf16[96,384]{1,0:T(8,128)(2,1)S(1)}, bf16[96,384]{1,0:T(8,128)(2,1)}, u32[]{:S(2)}) copy-start(bf16[96,384]{1,0:T(8,128)(2,1)} %param.14) | copy-start | bytes 221188
  7.2 173.0 %all-gather.5.cloned.1.call-start = ((), (), s32[]{:S(2)}) async-start(), calls=%async_computation.7 | async-start | bytes 2359296 | tf_op jit(solution)/shard_map/all_gather | solution.py:86
  34.1 36.2 %copy-start.44 = (bf16[96,384]{1,0:T(8,128)(2,1)S(1)}, bf16[96,384]{1,0:T(8,128)(2,1)}, u32[]{:S(2)}) copy-start(bf16[96,384]{1,0:T(8,128)(2,1)} %param.13) | copy-start | bytes 221188
  101.9 1.6 copy-start.10
  103.0 1.1 copy-start.38
  103.5 1.3 copy-start.25
  103.5 1.5 copy-start.39
  104.8 4.4 copy-start.8
  107.4 1.9 copy-start.9
  109.3 3.3 copy-start.45
  112.5 67.6 %copy-start.6 = (bf16[2,512,6,64]{1,3,2,0:T(8,128)(2,1)}, bf16[2,512,6,64]{1,3,2,0:T(8,128)(2,1)S(1)}, u32[]{:S(2)}) copy-start(bf16[2,512,6,64]{1,3,2,0:T(8,128)(2,1)S(1)} %get-tuple-element.49) | copy-start | bytes 2359300
  112.6 90.2 %all-gather.7.cloned.1.call-start = ((), (), s32[]{:S(2)}) async-start(), calls=%async_computation.8 | async-start | bytes 2359296 | tf_op jit(solution)/shard_map/all_gather | solution.py:87
  144.1 2.4 copy-start.21
  144.7 2.0 copy-start.46
  146.6 177.1 %all-reduce.14.cloned.1.call-start = ((), (), s32[]{:S(2)}) async-start(), calls=%async_computation.9 | async-start | bytes 3145728 | tf_op jit(solution)/shard_map/psum | solution.py:104
  204.5 1.1 copy-start.29
  216.1 1.1 copy-start.23
  217.1 37.2 %copy-start.5 = (bf16[48,8,2,512]{3,1,2,0:T(8,128)(2,1)}, bf16[48,8,2,512]{3,1,2,0:T(8,128)(2,1)S(1)}, u32[]{:S(2)}) copy-start(bf16[48,8,2,512]{3,1,2,0:T(8,128)(2,1)S(1)} %copy.57) | copy-start | bytes 2359300
  217.1 2.3 copy-start.40
  217.2 37.1 %copy-start.41 = (bf16[576,96]{0,1:T(8,128)(2,1)S(1)}, bf16[576,96]{0,1:T(8,128)(2,1)}, u32[]{:S(2)}) copy-start(bf16[576,96]{0,1:T(8,128)(2,1)} %param.20) | copy-start | bytes 331780
  219.4 70.1 %copy-start.42 = (bf16[96,576]{1,0:T(8,128)(2,1)S(1)}, bf16[96,576]{1,0:T(8,128)(2,1)}, u32[]{:S(2)}) copy-start(bf16[96,576]{1,0:T(8,128)(2,1)} %param.19) | copy-start | bytes 331780
  219.4 141.9 %all-reduce.16.cloned.1.call-start = ((), (), s32[]{:S(2)}) async-start(), calls=%async_computation.10 | async-start | bytes 3145728 | tf_op jit(solution)/shard_map/psum | solution.py:123
  323.7 2.0 copy-start.1
  326.5 1.2 copy-start.37
  327.7 8.5 copy-start.30
  327.7 2.0 copy-start.31
  327.7 2.2 copy-start.35
  329.9 6.2 copy-start.36
  336.2 4.7 copy-start.47
  339.3 1.5 copy-start.48
  343.5 52.6 %all-gather.9.cloned.1.call-start = ((), (), s32[]{:S(2)}) async-start(), calls=%async_computation.11 | async-start | bytes 2359296 | tf_op jit(solution)/shard_map/all_gather | solution.py:147
  344.1 103.6 %all-gather.11.cloned.1.call-start = ((), (), s32[]{:S(2)}) async-start(), calls=%async_computation.12 | async-start | bytes 2359296 | tf_op jit(solution)/shard_map/all_gather | solution.py:148
  361.3 3.3 copy-start.7
  361.3 3.3 copy-start.32
  364.6 1.8 copy-start.18
  364.6 1.8 copy-start.24
  366.4 2.4 copy-start.2
  376.6 122.5 %reduce-scatter.16.cloned.1.call-start = ((), (), s32[]{:S(2)}) async-start(), calls=%async_computation.17 | async-start | bytes 1105920 | tf_op jit(solution)/shard_map/reduce_scatter | solution.py:226
  380.8 171.8 %reduce-scatter.18.cloned.1.call-start = ((), (), s32[]{:S(2)}) async-start(), calls=%async_computation.18 | async-start | bytes 1105920 | tf_op jit(solution)/shard_map/reduce_scatter | solution.py:229
  390.6 227.7 %reduce-scatter.20.cloned.1.call-start = ((), (), s32[]{:S(2)}) async-start(), calls=%async_computation.19 | async-start | bytes 1105920 | tf_op jit(solution)/shard_map/reduce_scatter | solution.py:232
  396.1 13.5 %copy-start.33 = (bf16[2,512,768]{2,1,0:T(8,128)(2,1)S(1)}, bf16[2,512,768]{2,1,0:T(8,128)(2,1)}, u32[]{:S(2)}) copy-start(bf16[2,512,768]{2,1,0:T(8,128)(2,1)} %param.21) | copy-start | bytes 4718596
  396.1 13.5 %copy-start.49 = (bf16[1024,576]{0,1:T(8,128)(2,1)S(1)}, bf16[1024,576]{0,1:T(8,128)(2,1)}, u32[]{:S(2)}) copy-start(bf16[1024,576]{0,1:T(8,128)(2,1)} %get-tuple-element.35) | copy-start | bytes 3538948
  412.1 270.9 %reduce-scatter.14.cloned.1.call-start = ((), (), s32[]{:S(2)}) async-start(), calls=%async_computation.16 | async-start | bytes 663552 | tf_op jit(solution)/shard_map/reduce_scatter | solution.py:220
  441.7 2.9 copy-start.3
  447.6 299.9 %reduce-scatter.12.cloned.1.call-start = ((), (), s32[]{:S(2)}) async-start(), calls=%async_computation.15 | async-start | bytes 663552 | tf_op jit(solution)/shard_map/reduce_scatter | solution.py:217
  458.9 1.9 copy-start.26
  459.9 0.9 copy-start.13
  462.7 349.5 %reduce-scatter.10.cloned.1.call-start = ((), (), s32[]{:S(2)}) async-start(), calls=%async_computation.14 | async-start | bytes 663552 | tf_op jit(solution)/shard_map/reduce_scatter | solution.py:214
  477.8 1.7 copy-start.19
  477.8 1.9 copy-start.20
  477.8 2.4 copy-start.34
  483.4 1.8 copy-start.27
  484.3 0.9 copy-start.16
  487.1 389.5 %reduce-scatter.8.cloned.1.call-start = ((), (), s32[]{:S(2)}) async-start(), calls=%async_computation.13 | async-start | bytes 663552 | tf_op jit(solution)/shard_map/reduce_scatter | solution.py:211
  487.1 3.1 copy-start.28
  489.4 0.9 copy-start.15
  492.1 419.1 %all-reduce.20.cloned.1.call-start = ((), (), s32[]{:S(2)}) async-start(), calls=%async_computation.21 | async-start | bytes 1327104 | tf_op jit(solution)/shard_map/psum | solution.py:238
  492.2 4.3 copy-start.12
  492.2 4.3 copy-start.17
  876.7 60.8 %all-reduce.18.cloned.1.call-start = ((), (), s32[]{:S(2)}) async-start(), calls=%async_computation.20 | async-start | bytes 6291456 | tf_op jit(solution)/shard_map/psum | solution.py:111
  877.0 2.5 copy-start.4
  877.0 2.5 copy-start.14
  877.0 2.6 copy-start.22
  (1 other events, 0.8 us)
Sparse Core Ops, SparseCore 0:
  112.7 24.6 all-gather.4
  146.7 25.1 all-gather.6
  219.5 17.6 all-reduce.13
  343.6 17.6 all-reduce.15
  362.7 28.3 all-gather.8
  392.5 27.1 all-gather.10
  423.1 63.3 reduce-scatter.15
  490.2 62.3 reduce-scatter.17
  555.9 62.3 reduce-scatter.19
  621.8 61.1 reduce-scatter.13
  686.3 61.1 reduce-scatter.11
  751.0 61.1 reduce-scatter.9
  815.5 61.1 reduce-scatter.7
  879.4 31.7 all-reduce.19
  914.0 23.4 all-reduce.17
where the time goes:
time: 987 us; the launch traced here: 980 us
  waiting for transfers between devices  437 us (44%)
  blocking collectives  292 us (30%)
  matrix products  132 us (13%)
  other arithmetic  58.6 us (6%)
  local copies, waits for them, and re-layouts  42.7 us (4%)
  between operations  16.5 us (2%)
    reduce_scatter x1, waiting for transfers between devices, on_device(): lax.psum_scatter(grad_down.astype(jnp.bfloat16), 'fsdp', scatter_dimensio...  65.8 us
    reduce_scatter x1, waiting for transfers between devices, on_device(): lax.psum_scatter(grad_key.astype(jnp.bfloat16), 'fsdp', scatter_dimension...  64.7 us
    reduce_scatter x1, waiting for transfers between devices, on_device(): lax.psum_scatter(grad_out.astype(jnp.bfloat16), 'fsdp', scatter_dimension...  64.7 us
    reduce_scatter x1, waiting for transfers between devices, on_device(): lax.psum_scatter(grad_value.astype(jnp.bfloat16), 'fsdp', scatter_dimensi...  64.5 us
    reduce_scatter x1, waiting for transfers between devices, on_device(): lax.psum_scatter(grad_query.astype(jnp.bfloat16), 'fsdp', scatter_dimensi...  64.5 us
    dot_general x21, matrix products, matmul(): return jnp.dot(a, b, preferred_element_type=jnp.float32)  54.8 us
    reduce_scatter x1, waiting for transfers between devices, on_device(): lax.psum_scatter(grad_up.astype(jnp.bfloat16), 'fsdp', scatter_dimension=...  53.5 us
    unnamed x2, blocking collectives  44.8 us
  transfers between devices with their start and end apart: 15, of which 9 were waited for; matrix products, arithmetic and copies ran while one was open for 17% of the time, Pallas kernels for 0%

commit v1 on v0

--- a/solution.py
+++ b/solution.py
@@ -2,7 +2,10 @@
 
 import jax
 import jax.numpy as jnp
+import numpy as np
 from jax import lax
+from jax.experimental import pallas as pl
+from jax.experimental.pallas import tpu as pltpu
 from jax.sharding import PartitionSpec as P
 
 HD = 64
@@ -46,7 +49,7 @@
     return jnp.dot(a, b, preferred_element_type=jnp.float32)
 
 
-def on_device(
+def on_device_blocks(
     tokens, gain_attn, w_query, w_key, w_value, w_out, gain_ffn, w_gate, w_up, w_down, cotangent
 ):
     full = (
@@ -259,7 +262,269 @@
     )
 
 
+swapped = ((0, 1), (1, 0))
+
+
+def gather_rows(shard, after=None):
+    if after is not None:
+        shard, _ = lax.optimization_barrier((shard, after))
+    count = lax.axis_size("fsdp")
+    me = lax.axis_index("fsdp")
+    whole = jnp.zeros((count,) + shard.shape, shard.dtype)
+    whole = lax.dynamic_update_index_in_dim(whole, shard, me, 0)
+    for step in range(1, count):
+        came = lax.ppermute(shard, "fsdp", [(i, i ^ step) for i in range(count)])
+        whole = lax.dynamic_update_index_in_dim(whole, came, me ^ step, 0)
+    return whole.reshape((-1,) + shard.shape[1:])
+
+
+def scatter_blocks(blocks):
+    count = lax.axis_size("fsdp")
+    me = lax.axis_index("fsdp")
+    total = lax.dynamic_index_in_dim(blocks, me, 0, keepdims=False).astype(jnp.float32)
+    for step in range(1, count):
+        give = lax.dynamic_index_in_dim(blocks, me ^ step, 0, keepdims=False)
+        came = lax.ppermute(give, "fsdp", [(i, i ^ step) for i in range(count)])
+        total = total + came.astype(jnp.float32)
+    low = total.astype(blocks.dtype)
+    other = lax.ppermute(low, "ctx", swapped)
+    return low.astype(jnp.float32) + other.astype(jnp.float32)
+
+
+def scatter_rows(grad):
+    count = lax.axis_size("fsdp")
+    return scatter_blocks(grad.astype(jnp.bfloat16).reshape(count, -1, grad.shape[1]))
+
+
+def sum_tp(part):
+    part = part.astype(jnp.bfloat16)
+    other = lax.ppermute(part, "tp", swapped)
+    return part.astype(jnp.float32) + other.astype(jnp.float32)
+
+
+def take_sequence(blocks):
+    c = lax.axis_index("ctx")
+    own = lax.dynamic_index_in_dim(blocks, c, 0, keepdims=False)
+    give = lax.dynamic_index_in_dim(blocks, 1 - c, 0, keepdims=False)
+    return jnp.concatenate([own, lax.ppermute(give, "ctx", swapped)], axis=0)
+
+
+def give_back(own, came):
+    c = lax.axis_index("ctx")
+    return jnp.where(c == 0, jnp.stack([own, came]), jnp.stack([came, own]))
+
+
+def dot(a, b, over):
+    return lax.dot_general(a, b, (over, ((), ())), preferred_element_type=jnp.float32)
+
+
+def turn(u):
+    lane = lax.broadcasted_iota(jnp.int32, u.shape, 1)
+    return jnp.where(lane % HD < HD // 2, -pltpu.roll(u, 96, 1), pltpu.roll(u, 32, 1))
+
+
+def attend_kernel(h_ref, w_ref, cos_ref, sin_ref, q_ref, k_ref, v_ref, o_ref, lse_ref, *, tile):
+    rows = h_ref.shape[0]
+    raw = jnp.dot(h_ref[...], w_ref[...], preferred_element_type=jnp.float32)
+    cosine, sine = cos_ref[...], sin_ref[...]
+    q_raw, k_raw = raw[:, :128], raw[:, 128:256]
+    q_ref[...] = (q_raw * cosine + turn(q_raw) * sine).astype(jnp.bfloat16)
+    k_ref[...] = (k_raw * cosine + turn(k_raw) * sine).astype(jnp.bfloat16)
+    v = raw[:, 256:]
+    v_ref[...] = v.astype(jnp.bfloat16)
+    v_turned = v.T.astype(jnp.bfloat16)
+    k = k_ref[...]
+    lane = lax.broadcasted_iota(jnp.int32, (tile, 128), 1)
+    for start in range(0, rows, tile):
+        at = slice(start, start + tile)
+        q = q_ref[at, :] * jnp.bfloat16(HD ** (-0.5))
+        outs = []
+        for head in range(2):
+            mine = (lane // HD) == head
+            qm = jnp.where(mine, q, jnp.zeros_like(q))
+            s = dot(k, qm, ((1,), (1,)))
+            top = jnp.max(s, axis=0, keepdims=True)
+            e = jnp.exp(s - top)
+            total = jnp.sum(e, axis=0, keepdims=True)
+            lse_ref[0, head : head + 1, at] = top + jnp.log(total)
+            vh = v_turned[head * HD : (head + 1) * HD]
+            outs.append(dot(vh, e.astype(jnp.bfloat16), ((1,), (0,))) / total)
+        o_ref[at, :] = jnp.concatenate(outs, axis=0).T.astype(jnp.bfloat16)
+
+
+def attend_back_kernel(
+    q_ref, k_ref, v_ref, o_ref, do_ref, lse_ref, cos_ref, sin_ref, out_ref, dk_ref, dv_ref, *, tile
+):
+    rows = q_ref.shape[0]
+    k, v = k_ref[...], v_ref[...]
+    k_turned = k.astype(jnp.float32).T.astype(jnp.bfloat16)
+    lane = lax.broadcasted_iota(jnp.int32, (tile, 128), 1)
+    dk_ref[...] = jnp.zeros_like(dk_ref)
+    dv_ref[...] = jnp.zeros_like(dv_ref)
+    for start in range(0, rows, tile):
+        at = slice(start, start + tile)
+        q = q_ref[at, :] * jnp.bfloat16(HD ** (-0.5))
+        do = do_ref[at, :]
+        prod = (do.astype(jnp.float32) * o_ref[at, :].astype(jnp.float32)).T
+        outs = []
+        for head in range(2):
+            mine = (lane // HD) == head
+            qm = jnp.where(mine, q, jnp.zeros_like(q))
+            dm = jnp.where(mine, do, jnp.zeros_like(do))
+            delta = jnp.sum(prod[head * HD : (head + 1) * HD], axis=0, keepdims=True)
+            p = jnp.exp(dot(k, qm, ((1,), (1,))) - lse_ref[0, head : head + 1, at])
+            ds = (p * (dot(v, dm, ((1,), (1,))) - delta)).astype(jnp.bfloat16)
+            dv_ref[...] += dot(p.astype(jnp.bfloat16), dm, ((1,), (0,)))
+            dk_ref[...] += dot(ds, qm, ((1,), (0,)))
+            outs.append(dot(k_turned[head * HD : (head + 1) * HD], ds, ((1,), (0,))))
+        dq = jnp.concatenate(outs, axis=0).T * (HD ** (-0.5))
+        dq = dq * cos_ref[at, :] - turn(dq) * sin_ref[at, :]
+        out_ref[at, :128] = dq.astype(jnp.bfloat16)
+    dk = dk_ref[...]
+    out_ref[:, 128:256] = (dk * cos_ref[...] - turn(dk) * sin_ref[...]).astype(jnp.bfloat16)
+    out_ref[:, 256:] = dv_ref[...].astype(jnp.bfloat16)
+
+
+def attend(h_one, w_pairs, cosine, sine):
+    rows, model = h_one.shape
+    pairs = w_pairs.shape[1] // 384
+    width = pairs * 128
+    column = pl.BlockSpec((rows, 128), lambda i: (0, i))
+    table = pl.BlockSpec((rows, 128), lambda i: (0, 0))
+    low = jax.ShapeDtypeStruct((rows, width), jnp.bfloat16)
+    return pl.pallas_call(
+        partial(attend_kernel, tile=min(512, rows)),
+        grid=(pairs,),
+        in_specs=[
+            pl.BlockSpec((rows, model), lambda i: (0, 0)),
+            pl.BlockSpec((model, 384), lambda i: (0, i)),
+            table,
+            table,
+        ],
+        out_specs=[column] * 4 + [pl.BlockSpec((1, 2, rows), lambda i: (i, 0, 0))],
+        out_shape=[low] * 4 + [jax.ShapeDtypeStruct((pairs, 2, rows), jnp.float32)],
+        compiler_params=pltpu.CompilerParams(vmem_limit_bytes=44 << 20),
+        cost_estimate=pl.CostEstimate(
+            flops=16 * 10**9, bytes_accessed=10**7, transcendentals=pairs * 2 * rows * rows
+        ),
+        name="attend",
+    )(h_one, w_pairs, cosine, sine)
+
+
+def attend_back(q, k, v, o, do, lse, cosine, sine):
+    rows, width = q.shape
+    pairs = width // 128
+    column = pl.BlockSpec((rows, 128), lambda i: (0, i))
+    table = pl.BlockSpec((rows, 128), lambda i: (0, 0))
+    return pl.pallas_call(
+        partial(attend_back_kernel, tile=min(512, rows)),
+        grid=(pairs,),
+        in_specs=[column] * 5 + [pl.BlockSpec((1, 2, rows), lambda i: (i, 0, 0)), table, table],
+        out_specs=pl.BlockSpec((rows, 384), lambda i: (0, i)),
+        out_shape=jax.ShapeDtypeStruct((rows, 3 * width), jnp.bfloat16),
+        scratch_shapes=[pltpu.VMEM((rows, 128), jnp.float32)] * 2,
+        compiler_params=pltpu.CompilerParams(vmem_limit_bytes=44 << 20),
+        cost_estimate=pl.CostEstimate(
+            flops=30 * 10**9, bytes_accessed=10**7, transcendentals=pairs * 2 * rows * rows
+        ),
+        name="attend_back",
+    )(q, k, v, o, do, lse, cosine, sine)
+
+
+def rope_tables(rows):
+    angle = np.arange(2 * rows, dtype=np.float32)[:, None] * (
+        np.float32(1.0)
+        / np.float32(rope_base) ** (np.arange(0, HD, 2, dtype=np.float32) / np.float32(HD))
+    )[None, :].astype(np.float32)
+    tables = []
+    for values in (np.cos(angle), np.sin(angle)):
+        whole = jnp.asarray(np.tile(values.astype(np.float32), (1, 4)))
+        flipped = jnp.concatenate([whole[rows:], whole[:rows]], axis=0)
+        tables.append(jnp.where(lax.axis_index("ctx") == 0, whole, flipped))
+    return tables
+
+
+def on_device(
+    tokens, gain_attn, w_query, w_key, w_value, w_out, gain_ffn, w_gate, w_up, w_down, cotangent
+):
+    slots, rows, model = tokens.shape
+    part = w_query.shape[0]
+    width = w_query.shape[1]
+    pairs = width // 128
+    units = w_gate.shape[1]
+    packed = jnp.stack(
+        [w.reshape(part, pairs, 128) for w in (w_query, w_key, w_value)], axis=2
+    ).reshape(part, 3 * width)
+    gains = lax.all_gather(jnp.stack([gain_attn, gain_ffn]), "fsdp", axis=1, tiled=True)
+    gain_one, gain_two = gains[0].astype(jnp.float32), gains[1].astype(jnp.float32)
+    x = take_sequence(tokens).astype(jnp.float32)
+    qkv_w = gather_rows(packed)
+    out_w = gather_rows(w_out.T, qkv_w)
+    ffn_w = gather_rows(jnp.concatenate([w_gate, w_up], axis=1), qkv_w)
+    down_w = gather_rows(w_down.T, qkv_w)
+    cotangent, _ = lax.optimization_barrier((cotangent, qkv_w))
+    grad_low = take_sequence(cotangent)
+    grad_y = grad_low.astype(jnp.float32)
+    cosine, sine = rope_tables(rows)
+
+    normed_one, rstd_one = layer_norm(x)
+    h_one = (normed_one * gain_one).astype(jnp.bfloat16)
+    q, k, v, attended, lse = attend(h_one, qkv_w, cosine, sine)
+    x_two = x + sum_tp(dot(attended, out_w, ((1,), (1,))))
+    normed_two, rstd_two = layer_norm(x_two)
+    h_two = (normed_two * gain_two).astype(jnp.bfloat16)
+    both = matmul(h_two, ffn_w)
+    gate, up_part = both[:, :units], both[:, units:]
+    activated, gelu_back = jax.vjp(partial(jax.nn.gelu, approximate=False), gate)
+    hidden = (activated * up_part).astype(jnp.bfloat16)
+    output = (x_two + sum_tp(dot(hidden, down_w, ((1,), (1,))))).astype(jnp.bfloat16)
+    output = give_back(output[:rows], lax.ppermute(output[rows:], "ctx", swapped))
+
+    grad_hidden = matmul(grad_low, down_w)
+    grad_both = jnp.concatenate(
+        [
+            gelu_back(grad_hidden * up_part)[0].astype(jnp.bfloat16),
+            (grad_hidden * activated).astype(jnp.bfloat16),
+        ],
+        axis=1,
+    )
+    grad_h_two = sum_tp(dot(grad_both, ffn_w, ((1,), (1,))))
+    own_ffn = scatter_rows(dot(h_two, grad_both, ((0,), (0,))))
+    own_down = scatter_rows(dot(grad_low, hidden, ((0,), (0,))))
+    grad_gain_ffn = jnp.sum(grad_h_two * normed_two, axis=0)
+    grad_x_two = grad_y + norm_back(grad_h_two * gain_two, normed_two, rstd_two)
+    branch_low = grad_x_two.astype(jnp.bfloat16)
+    own_out = scatter_rows(dot(branch_low, attended, ((0,), (0,))))
+    grad_att = matmul(branch_low, out_w).astype(jnp.bfloat16)
+    grad_qkv = attend_back(q, k, v, attended, grad_att, lse, cosine, sine)
+    grad_h_one = sum_tp(dot(grad_qkv, qkv_w, ((1,), (1,))))
+    own_qkv = scatter_rows(dot(h_one, grad_qkv, ((0,), (0,))))
+    grad_gain_attn = jnp.sum(grad_h_one * normed_one, axis=0)
+    grad_x = grad_x_two + norm_back(grad_h_one * gain_one, normed_one, rstd_one)
+    came = lax.ppermute(grad_x[rows:].astype(jnp.bfloat16), "ctx", swapped).astype(jnp.float32)
+    grad_tokens = give_back(grad_x[:rows], came)
+    own_gains = scatter_blocks(
+        jnp.stack([grad_gain_attn, grad_gain_ffn]).reshape(2, -1, part).transpose(1, 0, 2)
+    )
+    own_qkv = own_qkv.reshape(part, pairs, 3, 128)
+    return (
+        output,
+        grad_tokens,
+        own_gains[0],
+        own_qkv[:, :, 0].reshape(part, width),
+        own_qkv[:, :, 1].reshape(part, width),
+        own_qkv[:, :, 2].reshape(part, width),
+        own_out.T,
+        own_gains[1],
+        own_ffn[:, :units],
+        own_ffn[:, units:],
+        own_down.T,
+    )
+
+
 def solution(mesh):
+    whole = mesh.shape["ctx"] == 2 and mesh.shape["tp"] == 2
+    step = on_device if whole and mesh.shape["fsdp"] == 8 else on_device_blocks
     placed = (
         P(None, ("fsdp", "ctx"), None),
         P("fsdp"),
@@ -274,7 +539,7 @@
         P(None, ("fsdp", "ctx"), None),
     )
     return jax.shard_map(
-        on_device,
+        step,
         mesh=mesh,
         in_specs=placed,
         out_specs=(

time: 987 us -> 460 us (0.47)
  waiting for transfers between devices: 437 us -> 141 us
  blocking collectives: 292 us -> 28.8 us
  starting transfers between devices: 1.63 us -> 154 us
  matrix products: 132 us -> 28.4 us
  Pallas kernels: 0 us -> 34.1 us
  other arithmetic: 58.6 us -> 38.7 us
  local copies, waits for them, and re-layouts: 42.7 us -> 23.9 us
  between operations: 16.5 us -> 2.27 us
    reduce_scatter x7 -> x0, waiting for transfers between devices: 378 us -> none  [the longest x1 65.8 us: on_device(): lax.psum_scatter(grad_down.astype(jnp.bfloat16), 'fsdp', scatter_dimensio...]
    all_gather x9 -> x1, blocking collectives: 242 us -> 28.8 us  [on_device(): lax.all_gather(jnp.stack([gain_attn, gain_ffn]), 'fsdp', axis=1, tiled=True)]
    ppermute x0 -> x76, starting transfers between devices: none -> 154 us  [the longest x35 88 us: scatter_blocks(): came = lax.ppermute(give, 'fsdp', [(i, i ^ step) for i in range(count)])]
    ppermute x0 -> x76, waiting for transfers between devices: none -> 141 us  [the longest x28 75.2 us: gather_rows(): came = lax.ppermute(shard, 'fsdp', [(i, i ^ step) for i in range(count)])]
    dot_general x6 -> x8, matrix products: 77.6 us -> 18.2 us  [dot(): lax.dot_general(a, b, (over, ((), ())), preferred_element_type=jnp.float32)]
    psum x4 -> x0, waiting for transfers between devices: 58.3 us -> none  [the longest x1 28.7 us: on_device(): lax.psum(pieces[1].astype(jnp.bfloat16), 'ctx').astype(jnp.float32)]
    unnamed x2 -> x0, blocking collectives: 44.8 us -> none
    dot_general x21 -> x3, matrix products: 54.8 us -> 10.2 us  [matmul(): return jnp.dot(a, b, preferred_element_type=jnp.float32)]
  transfers between devices with their start and end apart: 15 -> 76, of which waited for: 9 -> 27; matrix products, arithmetic and copies ran while one was open for 17% -> 9% of each run, Pallas kernels for 0% -> 4%
where the time goes in v1:
time: 460 us; the launch traced here: 451 us
  starting transfers between devices  154 us (33%)
  waiting for transfers between devices  141 us (31%)
  other arithmetic  38.7 us (8%)
  Pallas kernels  34.1 us (7%)
  blocking collectives  28.8 us (6%)
  matrix products  28.4 us (6%)
  local copies, waits for them, and re-layouts  23.9 us (5%)
    ppermute x35, starting transfers between devices, scatter_blocks(): came = lax.ppermute(give, 'fsdp', [(i, i ^ step) for i in range(count)])  88 us
    ppermute x28, waiting for transfers between devices, gather_rows(): came = lax.ppermute(shard, 'fsdp', [(i, i ^ step) for i in range(count)])  75.2 us
    ppermute x28, starting transfers between devices, gather_rows(): came = lax.ppermute(shard, 'fsdp', [(i, i ^ step) for i in range(count)])  52.9 us
    ppermute x35, waiting for transfers between devices, scatter_blocks(): came = lax.ppermute(give, 'fsdp', [(i, i ^ step) for i in range(count)])  35.1 us
    all_gather x1, blocking collectives, on_device(): lax.all_gather(jnp.stack([gain_attn, gain_ffn]), 'fsdp', axis=1, tiled=True)  28.8 us
    ppermute x5, waiting for transfers between devices, scatter_blocks(): other = lax.ppermute(low, 'ctx', swapped)  27.8 us
    dot_general x8, matrix products, dot(): lax.dot_general(a, b, (over, ((), ())), preferred_element_type=jnp.float32)  18.2 us
    pallas_call x1, Pallas kernels, attend_back(): pl.pallas_call(partial(attend_back_kernel, tile=min(512, rows)), grid=(pa...  17.8 us
  transfers between devices with their start and end apart: 76, of which 27 were waited for; matrix products, arithmetic and copies ran while one was open for 9% of the time, Pallas kernels for 4%

profile of v1, /device:TPU:0, one launch (start us, length us, event | category | flops | bytes accessed | tf_op | source)
XLA Modules:
  0.0 451.2 jit_solution(5874536875361468266)
XLA Ops:
  5.0 6.0 %collective-permute-start.7 = (bf16[96,1152]{1,0:T(8,128)(2,1)}, bf16[96,1152]{1,0:T(8,128)(2,1)S(1)}, u32[]{:S(2)}, u32[]{:S(2)}) collective-permute-start(bf16[96,1152]{1,0:T(8,128)(2,1)} %reshape.122), channel_id=1, source_target_pairs={{0,28},{4,24},{8,20},{12,16},{16,12},{20,8},{24,4},{28,0},{1,29},{... | collective-permute-start | bytes 663560 | tf_op jit(solution)/shard_map/ppermute | solution.py:276
  15.9 28.8 %all-gather = bf16[8,96,2]{1,2,0:T(2,128)(2,1)S(1)} all-gather(bf16[1,96,2]{1,2,0:T(2,128)(2,1)S(1)} %maximum_bitcast_fusion), channel_id=1, replica_groups=mesh['fsdp'=8,'ctx'=2,'tp'=2] {'fsdp'}, dimensions={0}, use_global_device_ids=true | all-gather | bytes 3456 | tf_op jit(solution)/shard_map/all_gather | solution.py:458
  46.5 13.9 %collective-permute-start.2 = (bf16[96,1152]{1,0:T(8,128)(2,1)}, bf16[96,1152]{1,0:T(8,128)(2,1)S(1)}, u32[]{:S(2)}, u32[]{:S(2)}) collective-permute-start(bf16[96,1152]{1,0:T(8,128)(2,1)} %reshape.122), channel_id=1, source_target_pairs={{0,8},{4,12},{8,0},{12,4},{16,24},{20,28},{24,16},{28,20},{1,9},{5... | collective-permute-start | bytes 663560 | tf_op jit(solution)/shard_map/ppermute | solution.py:276
  61.3 5.0 %collective-permute-done.2 = bf16[96,1152]{1,0:T(8,128)(2,1)S(1)} collective-permute-done((bf16[96,1152]{1,0:T(8,128)(2,1)}, bf16[96,1152]{1,0:T(8,128)(2,1)S(1)}, u32[]{:S(2)}, u32[]{:S(2)}) %collective-permute-start.2) | collective-permute-done | bytes 221216 | tf_op jit(solution)/shard_map/ppermute | solution.py:276
  67.8 5.6 %collective-permute-done.3 = bf16[96,1152]{1,0:T(8,128)(2,1)S(1)} collective-permute-done((bf16[96,1152]{1,0:T(8,128)(2,1)}, bf16[96,1152]{1,0:T(8,128)(2,1)S(1)}, u32[]{:S(2)}, u32[]{:S(2)}) %collective-permute-start.3) | collective-permute-done | bytes 221216 | tf_op jit(solution)/shard_map/ppermute | solution.py:276
  78.0 3.0 collective-permute-start.14
  82.3 2.9 collective-permute-start.12
  85.7 5.1 %collective-permute-done.8 = bf16[96,384]{1,0:T(8,128)(2,1)S(1)} collective-permute-done((bf16[96,384]{1,0:T(8,128)(2,1)S(1)}, bf16[96,384]{1,0:T(8,128)(2,1)S(1)}, u32[]{:S(2)}, u32[]{:S(2)}) %collective-permute-start.8) | collective-permute-done | bytes 73760 | tf_op jit(solution)/shard_map/ppermute | solution.py:276
  91.6 3.6 collective-permute-done.9
  95.4 5.9 %collective-permute-done.10 = bf16[96,384]{1,0:T(8,128)(2,1)S(1)} collective-permute-done((bf16[96,384]{1,0:T(8,128)(2,1)S(1)}, bf16[96,384]{1,0:T(8,128)(2,1)S(1)}, u32[]{:S(2)}, u32[]{:S(2)}) %collective-permute-start.10) | collective-permute-done | bytes 73760 | tf_op jit(solution)/shard_map/ppermute | solution.py:276
  101.8 5.4 %collective-permute-done.11 = bf16[96,384]{1,0:T(8,128)(2,1)S(1)} collective-permute-done((bf16[96,384]{1,0:T(8,128)(2,1)S(1)}, bf16[96,384]{1,0:T(8,128)(2,1)S(1)}, u32[]{:S(2)}, u32[]{:S(2)}) %collective-permute-start.11) | collective-permute-done | bytes 73760 | tf_op jit(solution)/shard_map/ppermute | solution.py:276
  108.0 4.3 collective-permute-start.28
  112.8 4.6 %collective-permute-done.23 = bf16[96,576]{1,0:T(8,128)(2,1)S(1)} collective-permute-done((bf16[96,576]{1,0:T(8,128)(2,1)S(1)}, bf16[96,576]{1,0:T(8,128)(2,1)S(1)}, u32[]{:S(2)}, u32[]{:S(2)}) %collective-permute-start.23) | collective-permute-done | bytes 110624 | tf_op jit(solution)/shard_map/ppermute | solution.py:276
  117.4 2.8 collective-permute-start.24
  120.2 2.8 collective-permute-done.24
  125.1 8.1 %collective-permute-done.25 = bf16[96,576]{1,0:T(8,128)(2,1)S(1)} collective-permute-done((bf16[96,576]{1,0:T(8,128)(2,1)S(1)}, bf16[96,576]{1,0:T(8,128)(2,1)S(1)}, u32[]{:S(2)}, u32[]{:S(2)}) %collective-permute-start.25) | collective-permute-done | bytes 110624 | tf_op jit(solution)/shard_map/ppermute | solution.py:276
  133.2 7.1 %collective-permute-done.26 = bf16[96,576]{1,0:T(8,128)(2,1)S(1)} collective-permute-done((bf16[96,576]{1,0:T(8,128)(2,1)S(1)}, bf16[96,576]{1,0:T(8,128)(2,1)S(1)}, u32[]{:S(2)}, u32[]{:S(2)}) %collective-permute-start.26) | collective-permute-done | bytes 110624 | tf_op jit(solution)/shard_map/ppermute | solution.py:276
  140.3 2.4 collective-permute-start.22
  142.7 2.7 collective-permute-start.21
  145.9 6.4 %collective-permute-done.16 = bf16[96,1152]{1,0:T(8,128)(2,1)S(1)} collective-permute-done((bf16[96,1152]{1,0:T(8,128)(2,1)S(1)}, bf16[96,1152]{1,0:T(8,128)(2,1)S(1)}, u32[]{:S(2)}, u32[]{:S(2)}) %collective-permute-start.16) | collective-permute-done | bytes 221216 | tf_op jit(solution)/shard_map/ppermute | solution.py:276
  152.4 2.7 collective-permute-start.17
  155.1 8.5 %collective-permute-done.17 = bf16[96,1152]{1,0:T(8,128)(2,1)S(1)} collective-permute-done((bf16[96,1152]{1,0:T(8,128)(2,1)S(1)}, bf16[96,1152]{1,0:T(8,128)(2,1)S(1)}, u32[]{:S(2)}, u32[]{:S(2)}) %collective-permute-start.17) | collective-permute-done | bytes 221216 | tf_op jit(solution)/shard_map/ppermute | solution.py:276
  163.7 6.8 %collective-permute-done.18 = bf16[96,1152]{1,0:T(8,128)(2,1)S(1)} collective-permute-done((bf16[96,1152]{1,0:T(8,128)(2,1)S(1)}, bf16[96,1152]{1,0:T(8,128)(2,1)S(1)}, u32[]{:S(2)}, u32[]{:S(2)}) %collective-permute-start.18) | collective-permute-done | bytes 221216 | tf_op jit(solution)/shard_map/ppermute | solution.py:276
  172.4 16.3 %attend.1 = (bf16[1024,384]{1,0:T(8,128)(2,1)S(1)}, bf16[1024,384]{1,0:T(8,128)(2,1)S(1)}, bf16[1024,384]{1,0:T(8,128)(2,1)S(1)}, bf16[1024,384]{1,0:T(8,128)(2,1)S(1)}, f32[3,2,1024]{2,1,0:T(2,128)S(1)}) custom-call(bf16[1024,768]{1,0:T(8,128)(2,1)S(1)} %fusion.6.h_ref, bf16[768,1152]{1,0:T(8,128)(2,1)S(1)} %bitcast.227, ...), custom_call_target="tpu_custom_call" | custom-call | flops 16000000000 | bytes 10000000 | tf_op jit(solution)/shard_map/attend/pallas_call | solution.py:395
  190.0 3.2 collective-permute-done.15
  194.5 2.4 fusion.82
  196.9 6.8 %add_convert_fusion.1 = (bf16[1024,576]{1,0:T(8,128)(2,1)S(1)}, f32[1024,576]{1,0:T(8,128)S(1)}, f32[1024,576]{1,0:T(8,128)S(1)}) fusion(f32[1024,1152]{1,0:T(8,128)S(1)} %fusion.82, bf16[768,576]{1,0:T(8,128)(2,1)S(1)} %bitcast.241, bf16[512,768]{1,0:T(8,128)(2,1)S(1)} %collective-permute-done.32, bf16[512,768]{1,0:T(8,128)(2,1)S(1)} %get-tuple-element.64), kind=kOutput, calls=%fused_computation.33 | convolution fusion | flops 952172544 | bytes 13074432 | tf_op jit(solution)/shard_map/dot_general | solution.py:49
  203.7 12.5 %multiply_convert_fusion.1 = (bf16[1024,576]{1,0:T(8,128)(2,1)S(1)}, bf16[1024,576]{1,0:T(8,128)(2,1)S(1)}) fusion(f32[1024,576]{1,0:T(8,128)S(1)} %get-tuple-element.92, f32[1024,576]{1,0:T(8,128)S(1)} %get-tuple-element.41, f32[1024,1152]{1,0:T(8,128)S(1)} %fusion.82), kind=kLoop, calls=%fused_computation.32 | loop fusion | flops 3538944 | bytes 11796480 | tf_op jit(solution)/shard_map/convert_element_type | solution.py:487
  216.3 3.4 convolution_convert_fusion.5
  219.7 3.6 convolution_convert_fusion
  225.4 2.2 copy.59
  230.0 2.6 collective-permute-start.74
  239.7 10.8 %collective-permute-start.69 = (bf16[96,576]{1,0:T(8,128)(2,1)S(1)}, bf16[96,576]{1,0:T(8,128)(2,1)S(1)}, u32[]{:S(2)}, u32[]{:S(2)}) collective-permute-start(bf16[96,576]{1,0:T(8,128)(2,1)S(1)} %get-tuple-element.74), channel_id=1, source_target_pairs={{0,8},{4,12},{8,0},{12,4},{16,24},{20,28},{24,16},{28,20},{1,9},{5... | collective-permute-start | bytes 331784 | tf_op jit(solution)/shard_map/ppermute | solution.py:287
  250.7 3.7 collective-permute-done.72
  254.4 2.7 collective-permute-start.66
  260.2 6.7 %collective-permute-done.69 = bf16[96,576]{1,0:T(8,128)(2,1)S(1)} collective-permute-done((bf16[96,576]{1,0:T(8,128)(2,1)S(1)}, bf16[96,576]{1,0:T(8,128)(2,1)S(1)}, u32[]{:S(2)}, u32[]{:S(2)}) %collective-permute-start.69) | collective-permute-done | bytes 110624 | tf_op jit(solution)/shard_map/ppermute | solution.py:287
  266.9 2.3 collective-permute-start.62
  269.2 13.3 %collective-permute-start.61 = (bf16[96,1152]{1,0:T(8,128)(2,1)S(1)}, bf16[96,1152]{1,0:T(8,128)(2,1)S(1)}, u32[]{:S(2)}, u32[]{:S(2)}) collective-permute-start(bf16[96,1152]{1,0:T(8,128)(2,1)S(1)} %get-tuple-element.54), channel_id=1, source_target_pairs={{0,8},{4,12},{8,0},{12,4},{16,24},{20,28},{24,16},{28,20},{1,9},{5... | collective-permute-start | bytes 663560 | tf_op jit(solution)/shard_map/ppermute | solution.py:287
  283.6 7.0 %collective-permute-done.64 = bf16[96,1152]{1,0:T(8,128)(2,1)S(1)} collective-permute-done((bf16[96,1152]{1,0:T(8,128)(2,1)S(1)}, bf16[96,1152]{1,0:T(8,128)(2,1)S(1)}, u32[]{:S(2)}, u32[]{:S(2)}) %collective-permute-start.64) | collective-permute-done | bytes 221216 | tf_op jit(solution)/shard_map/ppermute | solution.py:287
  290.5 2.7 collective-permute-done.63
  297.7 2.6 collective-permute-start.67
  301.0 4.4 collective-permute-done.67
  308.1 2.6 multiply_add_fusion
  314.1 17.8 %attend_back.1 = bf16[1024,1152]{1,0:T(8,128)(2,1)S(1)} custom-call(bf16[1024,384]{1,0:T(8,128)(2,1)S(1)} %copy-done.7, bf16[1024,384]{1,0:T(8,128)(2,1)S(1)} %copy-done.9, bf16[1024,384]{1,0:T(8,128)(2,1)S(1)} %copy-done.11, bf16[1024,384]{1,0:T(8,128)(2,1)S(1)} %copy-done.1, bf16[1024,384]{1,0:T(8,128)(2,1)S(1)} %convolution_convert_fusion.7.do_ref, ...), custom_call_target="tpu_custom_call" | custom-call | flops 30000001024 | bytes 10000000 | tf_op jit(solution)/shard_map/attend_back/pallas_call | solution.py:419
  331.9 3.4 convolution_convert_fusion.4
  335.3 2.2 convolution_convert_fusion.1
  339.4 2.5 collective-permute-start.58
  341.9 2.1 collective-permute-start.57
  344.0 3.0 collective-permute-start.55
  347.6 2.5 collective-permute-start.53
  350.7 2.2 collective-permute-done.56
  352.9 2.4 collective-permute-start.50
  355.3 2.1 collective-permute-start.49
  358.8 3.3 collective-permute-start.47
  364.1 16.2 %collective-permute-start.45 = (bf16[96,1152]{1,0:T(8,128)(2,1)S(1)}, bf16[96,1152]{1,0:T(8,128)(2,1)S(1)}, u32[]{:S(2)}, u32[]{:S(2)}) collective-permute-start(bf16[96,1152]{1,0:T(8,128)(2,1)S(1)} %get-tuple-element.61), channel_id=1, source_target_pairs={{0,8},{4,12},{8,0},{12,4},{16,24},{20,28},{24,16},{28,20},{1,9},{5... | collective-permute-start | bytes 663560 | tf_op jit(solution)/shard_map/ppermute | solution.py:287
  380.3 8.9 %collective-permute-done.48 = bf16[96,1152]{1,0:T(8,128)(2,1)S(1)} collective-permute-done((bf16[96,1152]{1,0:T(8,128)(2,1)S(1)}, bf16[96,1152]{1,0:T(8,128)(2,1)S(1)}, u32[]{:S(2)}, u32[]{:S(2)}) %collective-permute-start.48) | collective-permute-done | bytes 221216 | tf_op jit(solution)/shard_map/ppermute | solution.py:287
  396.1 13.3 %collective-permute-done.59 = bf16[96,384]{1,0:T(8,128)(2,1)S(1)} collective-permute-done((bf16[96,384]{1,0:T(8,128)(2,1)S(1)}, bf16[96,384]{1,0:T(8,128)(2,1)S(1)}, u32[]{:S(2)}, u32[]{:S(2)}) %collective-permute-start.59) | collective-permute-done | bytes 73760 | tf_op jit(solution)/shard_map/ppermute | solution.py:290
  415.3 4.3 fusion.11
  421.2 2.1 collective-permute-start.38
  424.2 3.6 fusion.10
  427.9 2.9 collective-permute-start.40
  431.9 2.8 collective-permute-start.42
  436.0 2.9 maximum_select_fusion.1
  439.9 8.4 %collective-permute-done.43 = f32[2,96]{1,0:T(2,128)S(1)} collective-permute-done((f32[2,96]{1,0:T(2,128)S(1)}, f32[2,96]{1,0:T(2,128)S(1)}, u32[]{:S(2)}, u32[]{:S(2)}) %collective-permute-start.43) | collective-permute-done | bytes 800 | tf_op jit(solution)/shard_map/ppermute | solution.py:290
  (287 shorter events, 83.8 us)
Async XLA Ops:
  5.0 73.0 %collective-permute-start.7 = (bf16[96,1152]{1,0:T(8,128)(2,1)}, bf16[96,1152]{1,0:T(8,128)(2,1)S(1)}, u32[]{:S(2)}, u32[]{:S(2)}) collective-permute-start(bf16[96,1152]{1,0:T(8,128)(2,1)} %reshape.122), channel_id=1, source_target_pairs={{0,28},{4,24},{8,20},{12,16},{16,12},{20,8},{24,4},{28,0},{1,29},{... | collective-permute-start | bytes 663560 | tf_op jit(solution)/shard_map/ppermute | solution.py:276
  11.0 65.9 %collective-permute-start.6 = (bf16[96,1152]{1,0:T(8,128)(2,1)}, bf16[96,1152]{1,0:T(8,128)(2,1)}, u32[]{:S(2)}, u32[]{:S(2)}) collective-permute-start(bf16[96,1152]{1,0:T(8,128)(2,1)} %reshape.122), channel_id=1, source_target_pairs={{0,24},{4,28},{8,16},{12,20},{16,8},{20,12},{24,0},{28,4},{1,25},{... | collective-permute-start | bytes 663560 | tf_op jit(solution)/shard_map/ppermute | solution.py:276
  11.2 64.7 %collective-permute-start.5 = (bf16[96,1152]{1,0:T(8,128)(2,1)}, bf16[96,1152]{1,0:T(8,128)(2,1)}, u32[]{:S(2)}, u32[]{:S(2)}) collective-permute-start(bf16[96,1152]{1,0:T(8,128)(2,1)} %reshape.122), channel_id=1, source_target_pairs={{0,20},{4,16},{8,28},{12,24},{16,4},{20,0},{24,12},{28,8},{1,21},{... | collective-permute-start | bytes 663560 | tf_op jit(solution)/shard_map/ppermute | solution.py:276
  12.0 63.0 %collective-permute-start.4 = (bf16[96,1152]{1,0:T(8,128)(2,1)}, bf16[96,1152]{1,0:T(8,128)(2,1)}, u32[]{:S(2)}, u32[]{:S(2)}) collective-permute-start(bf16[96,1152]{1,0:T(8,128)(2,1)} %reshape.122), channel_id=1, source_target_pairs={{0,16},{4,20},{8,24},{12,28},{16,0},{20,4},{24,8},{28,12},{1,17},{... | collective-permute-start | bytes 663560 | tf_op jit(solution)/shard_map/ppermute | solution.py:276
  13.9 32.6 %collective-permute-start.1 = (bf16[96,1152]{1,0:T(8,128)(2,1)}, bf16[96,1152]{1,0:T(8,128)(2,1)}, u32[]{:S(2)}, u32[]{:S(2)}) collective-permute-start(bf16[96,1152]{1,0:T(8,128)(2,1)} %reshape.122), channel_id=1, source_target_pairs={{0,4},{4,0},{8,12},{12,8},{16,20},{20,16},{24,28},{28,24},{1,5},{5... | collective-permute-start | bytes 663560 | tf_op jit(solution)/shard_map/ppermute | solution.py:276
  46.5 19.9 %collective-permute-start.2 = (bf16[96,1152]{1,0:T(8,128)(2,1)}, bf16[96,1152]{1,0:T(8,128)(2,1)S(1)}, u32[]{:S(2)}, u32[]{:S(2)}) collective-permute-start(bf16[96,1152]{1,0:T(8,128)(2,1)} %reshape.122), channel_id=1, source_target_pairs={{0,8},{4,12},{8,0},{12,4},{16,24},{20,28},{24,16},{28,20},{1,9},{5... | collective-permute-start | bytes 663560 | tf_op jit(solution)/shard_map/ppermute | solution.py:276
  73.4 97.2 %collective-permute-start = (bf16[512,768]{1,0:T(8,128)(2,1)S(1)}, bf16[512,768]{1,0:T(8,128)(2,1)S(1)}, u32[]{:S(2)}, u32[]{:S(2)}) collective-permute-start(bf16[512,768]{1,0:T(8,128)(2,1)S(1)} %get-tuple-element.67), channel_id=1, source_target_pairs={{0,2},{2,0},{1,3},{3,1},{4,6},{6,4},{5,7},{7,5},{8,10},{10,8},{9,1... | collective-permute-start | bytes 2359304 | tf_op jit(solution)/shard_map/ppermute | solution.py:309
  78.0 34.4 %collective-permute-start.14 = (bf16[96,384]{1,0:T(8,128)(2,1)S(1)}, bf16[96,384]{1,0:T(8,128)(2,1)S(1)}, u32[]{:S(2)}, u32[]{:S(2)}) collective-permute-start(bf16[96,384]{1,0:T(8,128)(2,1)S(1)} %bitcast.257), channel_id=1, source_target_pairs={{0,28},{4,24},{8,20},{12,16},{16,12},{20,8},{24,4},{28,0},{1,29},{... | collective-permute-start | bytes 221192 | tf_op jit(solution)/shard_map/ppermute | solution.py:276
  81.0 31.3 %collective-permute-start.13 = (bf16[96,384]{1,0:T(8,128)(2,1)S(1)}, bf16[96,384]{1,0:T(8,128)(2,1)S(1)}, u32[]{:S(2)}, u32[]{:S(2)}) collective-permute-start(bf16[96,384]{1,0:T(8,128)(2,1)S(1)} %bitcast.258), channel_id=1, source_target_pairs={{0,24},{4,28},{8,16},{12,20},{16,8},{20,12},{24,0},{28,4},{1,25},{... | collective-permute-start | bytes 221192 | tf_op jit(solution)/shard_map/ppermute | solution.py:276
  82.3 25.7 %collective-permute-start.12 = (bf16[96,384]{1,0:T(8,128)(2,1)S(1)}, bf16[96,384]{1,0:T(8,128)(2,1)S(1)}, u32[]{:S(2)}, u32[]{:S(2)}) collective-permute-start(bf16[96,384]{1,0:T(8,128)(2,1)S(1)} %bitcast.259), channel_id=1, source_target_pairs={{0,20},{4,16},{8,28},{12,24},{16,4},{20,0},{24,12},{28,8},{1,21},{... | collective-permute-start | bytes 221192 | tf_op jit(solution)/shard_map/ppermute | solution.py:276
  107.2 38.4 %collective-permute-start.29 = (bf16[96,576]{1,0:T(8,128)(2,1)S(1)}, bf16[96,576]{1,0:T(8,128)(2,1)S(1)}, u32[]{:S(2)}, u32[]{:S(2)}) collective-permute-start(bf16[96,576]{1,0:T(8,128)(2,1)S(1)} %bitcast.250), channel_id=1, source_target_pairs={{0,28},{4,24},{8,20},{12,16},{16,12},{20,8},{24,4},{28,0},{1,29},{... | collective-permute-start | bytes 331784 | tf_op jit(solution)/shard_map/ppermute | solution.py:276
  108.0 37.5 %collective-permute-start.28 = (bf16[96,576]{1,0:T(8,128)(2,1)S(1)}, bf16[96,576]{1,0:T(8,128)(2,1)S(1)}, u32[]{:S(2)}, u32[]{:S(2)}) collective-permute-start(bf16[96,576]{1,0:T(8,128)(2,1)S(1)} %bitcast.251), channel_id=1, source_target_pairs={{0,24},{4,28},{8,16},{12,20},{16,8},{20,12},{24,0},{28,4},{1,25},{... | collective-permute-start | bytes 331784 | tf_op jit(solution)/shard_map/ppermute | solution.py:276
  112.3 30.4 %collective-permute-start.27 = (bf16[96,576]{1,0:T(8,128)(2,1)S(1)}, bf16[96,576]{1,0:T(8,128)(2,1)S(1)}, u32[]{:S(2)}, u32[]{:S(2)}) collective-permute-start(bf16[96,576]{1,0:T(8,128)(2,1)S(1)} %bitcast.252), channel_id=1, source_target_pairs={{0,20},{4,16},{8,28},{12,24},{16,4},{20,0},{24,12},{28,8},{1,21},{... | collective-permute-start | bytes 331784 | tf_op jit(solution)/shard_map/ppermute | solution.py:276
  123.1 10.1 %collective-permute-start.25 = (bf16[96,576]{1,0:T(8,128)(2,1)S(1)}, bf16[96,576]{1,0:T(8,128)(2,1)S(1)}, u32[]{:S(2)}, u32[]{:S(2)}) collective-permute-start(bf16[96,576]{1,0:T(8,128)(2,1)S(1)} %bitcast.255), channel_id=1, source_target_pairs={{0,12},{4,8},{8,4},{12,0},{16,28},{20,24},{24,20},{28,16},{1,13},{... | collective-permute-start | bytes 331784 | tf_op jit(solution)/shard_map/ppermute | solution.py:276
  133.2 7.1 %collective-permute-start.26 = (bf16[96,576]{1,0:T(8,128)(2,1)S(1)}, bf16[96,576]{1,0:T(8,128)(2,1)S(1)}, u32[]{:S(2)}, u32[]{:S(2)}) collective-permute-start(bf16[96,576]{1,0:T(8,128)(2,1)S(1)} %bitcast.256), channel_id=1, source_target_pairs={{0,16},{4,20},{8,24},{12,28},{16,0},{20,4},{24,8},{28,12},{1,17},{... | collective-permute-start | bytes 331784 | tf_op jit(solution)/shard_map/ppermute | solution.py:276
  140.3 49.6 %collective-permute-start.22 = (bf16[96,1152]{1,0:T(8,128)(2,1)S(1)}, bf16[96,1152]{1,0:T(8,128)(2,1)S(1)}, u32[]{:S(2)}, u32[]{:S(2)}) collective-permute-start(bf16[96,1152]{1,0:T(8,128)(2,1)S(1)} %pad_maximum_fusion.8), channel_id=1, source_target_pairs={{0,28},{4,24},{8,20},{12,16},{16,12},{20,8},{24,4},{28,0},{1,29},{... | collective-permute-start | bytes 663560 | tf_op jit(solution)/shard_map/ppermute | solution.py:276
  142.7 47.2 %collective-permute-start.21 = (bf16[96,1152]{1,0:T(8,128)(2,1)S(1)}, bf16[96,1152]{1,0:T(8,128)(2,1)S(1)}, u32[]{:S(2)}, u32[]{:S(2)}) collective-permute-start(bf16[96,1152]{1,0:T(8,128)(2,1)S(1)} %pad_maximum_fusion.8), channel_id=1, source_target_pairs={{0,24},{4,28},{8,16},{12,20},{16,8},{20,12},{24,0},{28,4},{1,25},{... | collective-permute-start | bytes 663560 | tf_op jit(solution)/shard_map/ppermute | solution.py:276
  145.5 44.4 %collective-permute-start.20 = (bf16[96,1152]{1,0:T(8,128)(2,1)S(1)}, bf16[96,1152]{1,0:T(8,128)(2,1)S(1)}, u32[]{:S(2)}, u32[]{:S(2)}) collective-permute-start(bf16[96,1152]{1,0:T(8,128)(2,1)S(1)} %pad_maximum_fusion.8), channel_id=1, source_target_pairs={{0,20},{4,16},{8,28},{12,24},{16,4},{20,0},{24,12},{28,8},{1,21},{... | collective-permute-start | bytes 663560 | tf_op jit(solution)/shard_map/ppermute | solution.py:276
  152.4 11.2 %collective-permute-start.17 = (bf16[96,1152]{1,0:T(8,128)(2,1)S(1)}, bf16[96,1152]{1,0:T(8,128)(2,1)S(1)}, u32[]{:S(2)}, u32[]{:S(2)}) collective-permute-start(bf16[96,1152]{1,0:T(8,128)(2,1)S(1)} %pad_maximum_fusion.8), channel_id=1, source_target_pairs={{0,8},{4,12},{8,0},{12,4},{16,24},{20,28},{24,16},{28,20},{1,9},{5... | collective-permute-start | bytes 663560 | tf_op jit(solution)/shard_map/ppermute | solution.py:276
  170.5 19.3 %collective-permute-start.19 = (bf16[96,1152]{1,0:T(8,128)(2,1)S(1)}, bf16[96,1152]{1,0:T(8,128)(2,1)S(1)}, u32[]{:S(2)}, u32[]{:S(2)}) collective-permute-start(bf16[96,1152]{1,0:T(8,128)(2,1)S(1)} %pad_maximum_fusion.8), channel_id=1, source_target_pairs={{0,16},{4,20},{8,24},{12,28},{16,0},{20,4},{24,8},{28,12},{1,17},{... | collective-permute-start | bytes 663560 | tf_op jit(solution)/shard_map/ppermute | solution.py:276
  170.6 26.3 %collective-permute-start.32 = (bf16[512,768]{1,0:T(8,128)(2,1)S(1)}, bf16[512,768]{1,0:T(8,128)(2,1)S(1)}, u32[]{:S(2)}, u32[]{:S(2)}) collective-permute-start(bf16[512,768]{1,0:T(8,128)(2,1)S(1)} %get-tuple-element.65), channel_id=1, source_target_pairs={{0,2},{2,0},{1,3},{3,1},{4,6},{6,4},{5,7},{7,5},{8,10},{10,8},{9,1... | collective-permute-start | bytes 2359304 | tf_op jit(solution)/shard_map/ppermute | solution.py:309
  229.1 10.1 %collective-permute-start.68 = (bf16[96,576]{1,0:T(8,128)(2,1)S(1)}, bf16[96,576]{1,0:T(8,128)(2,1)S(1)}, u32[]{:S(2)}, u32[]{:S(2)}) collective-permute-start(bf16[96,576]{1,0:T(8,128)(2,1)S(1)} %get-tuple-element.68), channel_id=1, source_target_pairs={{0,4},{4,0},{8,12},{12,8},{16,20},{20,16},{24,28},{28,24},{1,5},{5... | collective-permute-start | bytes 331784 | tf_op jit(solution)/shard_map/ppermute | solution.py:287
  230.0 9.7 %collective-permute-start.74 = (bf16[96,576]{1,0:T(8,128)(2,1)S(1)}, bf16[96,576]{1,0:T(8,128)(2,1)S(1)}, u32[]{:S(2)}, u32[]{:S(2)}) collective-permute-start(bf16[96,576]{1,0:T(8,128)(2,1)S(1)} %get-tuple-element.69), channel_id=1, source_target_pairs={{0,28},{4,24},{8,20},{12,16},{16,12},{20,8},{24,4},{28,0},{1,29},{... | collective-permute-start | bytes 331784 | tf_op jit(solution)/shard_map/ppermute | solution.py:287
  232.6 17.9 %collective-permute-start.73 = (bf16[96,576]{1,0:T(8,128)(2,1)S(1)}, bf16[96,576]{1,0:T(8,128)(2,1)S(1)}, u32[]{:S(2)}, u32[]{:S(2)}) collective-permute-start(bf16[96,576]{1,0:T(8,128)(2,1)S(1)} %get-tuple-element.70), channel_id=1, source_target_pairs={{0,24},{4,28},{8,16},{12,20},{16,8},{20,12},{24,0},{28,4},{1,25},{... | collective-permute-start | bytes 331784 | tf_op jit(solution)/shard_map/ppermute | solution.py:287
  234.5 19.9 %collective-permute-start.72 = (bf16[96,576]{1,0:T(8,128)(2,1)S(1)}, bf16[96,576]{1,0:T(8,128)(2,1)S(1)}, u32[]{:S(2)}, u32[]{:S(2)}) collective-permute-start(bf16[96,576]{1,0:T(8,128)(2,1)S(1)} %get-tuple-element.71), channel_id=1, source_target_pairs={{0,20},{4,16},{8,28},{12,24},{16,4},{20,0},{24,12},{28,8},{1,21},{... | collective-permute-start | bytes 331784 | tf_op jit(solution)/shard_map/ppermute | solution.py:287
  235.6 21.5 %collective-permute-start.71 = (bf16[96,576]{1,0:T(8,128)(2,1)S(1)}, bf16[96,576]{1,0:T(8,128)(2,1)S(1)}, u32[]{:S(2)}, u32[]{:S(2)}) collective-permute-start(bf16[96,576]{1,0:T(8,128)(2,1)S(1)} %get-tuple-element.72), channel_id=1, source_target_pairs={{0,16},{4,20},{8,24},{12,28},{16,0},{20,4},{24,8},{28,12},{1,17},{... | collective-permute-start | bytes 331784 | tf_op jit(solution)/shard_map/ppermute | solution.py:287
  239.2 20.9 %collective-permute-start.70 = (bf16[96,576]{1,0:T(8,128)(2,1)S(1)}, bf16[96,576]{1,0:T(8,128)(2,1)S(1)}, u32[]{:S(2)}, u32[]{:S(2)}) collective-permute-start(bf16[96,576]{1,0:T(8,128)(2,1)S(1)} %get-tuple-element.73), channel_id=1, source_target_pairs={{0,12},{4,8},{8,4},{12,0},{16,28},{20,24},{24,20},{28,16},{1,13},{... | collective-permute-start | bytes 331784 | tf_op jit(solution)/shard_map/ppermute | solution.py:287
  239.7 27.3 %collective-permute-start.69 = (bf16[96,576]{1,0:T(8,128)(2,1)S(1)}, bf16[96,576]{1,0:T(8,128)(2,1)S(1)}, u32[]{:S(2)}, u32[]{:S(2)}) collective-permute-start(bf16[96,576]{1,0:T(8,128)(2,1)S(1)} %get-tuple-element.74), channel_id=1, source_target_pairs={{0,8},{4,12},{8,0},{12,4},{16,24},{20,28},{24,16},{28,20},{1,9},{5... | collective-permute-start | bytes 331784 | tf_op jit(solution)/shard_map/ppermute | solution.py:287
  250.4 16.5 %collective-permute-start.60 = (bf16[96,1152]{1,0:T(8,128)(2,1)S(1)}, bf16[96,1152]{1,0:T(8,128)(2,1)S(1)}, u32[]{:S(2)}, u32[]{:S(2)}) collective-permute-start(bf16[96,1152]{1,0:T(8,128)(2,1)S(1)} %get-tuple-element.48), channel_id=1, source_target_pairs={{0,4},{4,0},{8,12},{12,8},{16,20},{20,16},{24,28},{28,24},{1,5},{5... | collective-permute-start | bytes 663560 | tf_op jit(solution)/shard_map/ppermute | solution.py:287
  254.4 14.8 %collective-permute-start.66 = (bf16[96,1152]{1,0:T(8,128)(2,1)S(1)}, bf16[96,1152]{1,0:T(8,128)(2,1)S(1)}, u32[]{:S(2)}, u32[]{:S(2)}) collective-permute-start(bf16[96,1152]{1,0:T(8,128)(2,1)S(1)} %get-tuple-element.49), channel_id=1, source_target_pairs={{0,28},{4,24},{8,20},{12,16},{16,12},{20,8},{24,4},{28,0},{1,29},{... | collective-permute-start | bytes 663560 | tf_op jit(solution)/shard_map/ppermute | solution.py:287
  257.0 25.5 %collective-permute-start.65 = (bf16[96,1152]{1,0:T(8,128)(2,1)S(1)}, bf16[96,1152]{1,0:T(8,128)(2,1)S(1)}, u32[]{:S(2)}, u32[]{:S(2)}) collective-permute-start(bf16[96,1152]{1,0:T(8,128)(2,1)S(1)} %get-tuple-element.50), channel_id=1, source_target_pairs={{0,24},{4,28},{8,16},{12,20},{16,8},{20,12},{24,0},{28,4},{1,25},{... | collective-permute-start | bytes 663560 | tf_op jit(solution)/shard_map/ppermute | solution.py:287
  260.1 30.4 %collective-permute-start.64 = (bf16[96,1152]{1,0:T(8,128)(2,1)S(1)}, bf16[96,1152]{1,0:T(8,128)(2,1)S(1)}, u32[]{:S(2)}, u32[]{:S(2)}) collective-permute-start(bf16[96,1152]{1,0:T(8,128)(2,1)S(1)} %get-tuple-element.51), channel_id=1, source_target_pairs={{0,20},{4,16},{8,28},{12,24},{16,4},{20,0},{24,12},{28,8},{1,21},{... | collective-permute-start | bytes 663560 | tf_op jit(solution)/shard_map/ppermute | solution.py:287
  266.9 26.4 %collective-permute-start.63 = (bf16[96,1152]{1,0:T(8,128)(2,1)S(1)}, bf16[96,1152]{1,0:T(8,128)(2,1)S(1)}, u32[]{:S(2)}, u32[]{:S(2)}) collective-permute-start(bf16[96,1152]{1,0:T(8,128)(2,1)S(1)} %get-tuple-element.52), channel_id=1, source_target_pairs={{0,16},{4,20},{8,24},{12,28},{16,0},{20,4},{24,8},{28,12},{1,17},{... | collective-permute-start | bytes 663560 | tf_op jit(solution)/shard_map/ppermute | solution.py:287
  266.9 28.4 %collective-permute-start.62 = (bf16[96,1152]{1,0:T(8,128)(2,1)S(1)}, bf16[96,1152]{1,0:T(8,128)(2,1)S(1)}, u32[]{:S(2)}, u32[]{:S(2)}) collective-permute-start(bf16[96,1152]{1,0:T(8,128)(2,1)S(1)} %get-tuple-element.53), channel_id=1, source_target_pairs={{0,12},{4,8},{8,4},{12,0},{16,28},{20,24},{24,20},{28,16},{1,13},{... | collective-permute-start | bytes 663560 | tf_op jit(solution)/shard_map/ppermute | solution.py:287
  269.2 27.4 %collective-permute-start.61 = (bf16[96,1152]{1,0:T(8,128)(2,1)S(1)}, bf16[96,1152]{1,0:T(8,128)(2,1)S(1)}, u32[]{:S(2)}, u32[]{:S(2)}) collective-permute-start(bf16[96,1152]{1,0:T(8,128)(2,1)S(1)} %get-tuple-element.54), channel_id=1, source_target_pairs={{0,8},{4,12},{8,0},{12,4},{16,24},{20,28},{24,16},{28,20},{1,9},{5... | collective-permute-start | bytes 663560 | tf_op jit(solution)/shard_map/ppermute | solution.py:287
  282.5 23.8 %collective-permute-start.33 = (bf16[1024,768]{1,0:T(8,128)(2,1)S(1)}, bf16[1024,768]{1,0:T(8,128)(2,1)S(1)}, u32[]{:S(2)}, u32[]{:S(2)}) collective-permute-start(bf16[1024,768]{1,0:T(8,128)(2,1)S(1)} %copy-done.18), channel_id=1, source_target_pairs={{0,1},{1,0},{2,3},{3,2},{4,5},{5,4},{6,7},{7,6},{8,9},{9,8},{10,11... | collective-permute-start | bytes 4718600 | tf_op jit(solution)/shard_map/ppermute | solution.py:301
  290.5 17.6 %collective-permute-start.30 = (bf16[1024,768]{1,0:T(8,128)(2,1)S(1)}, bf16[1024,768]{1,0:T(8,128)(2,1)S(1)}, u32[]{:S(2)}, u32[]{:S(2)}) collective-permute-start(bf16[1024,768]{1,0:T(8,128)(2,1)S(1)} %convolution_convert_fusion.2), channel_id=1, source_target_pairs={{0,1},{1,0},{2,3},{3,2},{4,5},{5,4},{6,7},{7,6},{8,9},{9,8},{10,11... | collective-permute-start | bytes 4718600 | tf_op jit(solution)/shard_map/ppermute | solution.py:301
  297.7 7.7 %collective-permute-start.67 = (bf16[96,1152]{1,0:T(8,128)(2,1)S(1)}, bf16[96,1152]{1,0:T(8,128)(2,1)S(1)}, u32[]{:S(2)}, u32[]{:S(2)}) collective-permute-start(bf16[96,1152]{1,0:T(8,128)(2,1)S(1)} %fusion.33), channel_id=1, source_target_pairs={{0,2},{2,0},{1,3},{3,1},{4,6},{6,4},{5,7},{7,5},{8,10},{10,8},{9,1... | collective-permute-start | bytes 663560 | tf_op jit(solution)/shard_map/ppermute | solution.py:290
  338.7 8.5 %collective-permute-start.52 = (bf16[96,384]{1,0:T(8,128)(2,1)S(1)}, bf16[96,384]{1,0:T(8,128)(2,1)S(1)}, u32[]{:S(2)}, u32[]{:S(2)}) collective-permute-start(bf16[96,384]{1,0:T(8,128)(2,1)S(1)} %get-tuple-element.75), channel_id=1, source_target_pairs={{0,4},{4,0},{8,12},{12,8},{16,20},{20,16},{24,28},{28,24},{1,5},{5... | collective-permute-start | bytes 221192 | tf_op jit(solution)/shard_map/ppermute | solution.py:287
  339.4 8.3 %collective-permute-start.58 = (bf16[96,384]{1,0:T(8,128)(2,1)S(1)}, bf16[96,384]{1,0:T(8,128)(2,1)S(1)}, u32[]{:S(2)}, u32[]{:S(2)}) collective-permute-start(bf16[96,384]{1,0:T(8,128)(2,1)S(1)} %get-tuple-element.76), channel_id=1, source_target_pairs={{0,28},{4,24},{8,20},{12,16},{16,12},{20,8},{24,4},{28,0},{1,29},{... | collective-permute-start | bytes 221192 | tf_op jit(solution)/shard_map/ppermute | solution.py:287
  341.9 8.2 %collective-permute-start.57 = (bf16[96,384]{1,0:T(8,128)(2,1)S(1)}, bf16[96,384]{1,0:T(8,128)(2,1)S(1)}, u32[]{:S(2)}, u32[]{:S(2)}) collective-permute-start(bf16[96,384]{1,0:T(8,128)(2,1)S(1)} %get-tuple-element.77), channel_id=1, source_target_pairs={{0,24},{4,28},{8,16},{12,20},{16,8},{20,12},{24,0},{28,4},{1,25},{... | collective-permute-start | bytes 221192 | tf_op jit(solution)/shard_map/ppermute | solution.py:287
  344.0 8.9 %collective-permute-start.56 = (bf16[96,384]{1,0:T(8,128)(2,1)S(1)}, bf16[96,384]{1,0:T(8,128)(2,1)S(1)}, u32[]{:S(2)}, u32[]{:S(2)}) collective-permute-start(bf16[96,384]{1,0:T(8,128)(2,1)S(1)} %get-tuple-element.78), channel_id=1, source_target_pairs={{0,20},{4,16},{8,28},{12,24},{16,4},{20,0},{24,12},{28,8},{1,21},{... | collective-permute-start | bytes 221192 | tf_op jit(solution)/shard_map/ppermute | solution.py:287
  344.0 11.3 %collective-permute-start.55 = (bf16[96,384]{1,0:T(8,128)(2,1)S(1)}, bf16[96,384]{1,0:T(8,128)(2,1)S(1)}, u32[]{:S(2)}, u32[]{:S(2)}) collective-permute-start(bf16[96,384]{1,0:T(8,128)(2,1)S(1)} %get-tuple-element.79), channel_id=1, source_target_pairs={{0,16},{4,20},{8,24},{12,28},{16,0},{20,4},{24,8},{28,12},{1,17},{... | collective-permute-start | bytes 221192 | tf_op jit(solution)/shard_map/ppermute | solution.py:287
  347.1 11.6 %collective-permute-start.54 = (bf16[96,384]{1,0:T(8,128)(2,1)S(1)}, bf16[96,384]{1,0:T(8,128)(2,1)S(1)}, u32[]{:S(2)}, u32[]{:S(2)}) collective-permute-start(bf16[96,384]{1,0:T(8,128)(2,1)S(1)} %get-tuple-element.80), channel_id=1, source_target_pairs={{0,12},{4,8},{8,4},{12,0},{16,28},{20,24},{24,20},{28,16},{1,13},{... | collective-permute-start | bytes 221192 | tf_op jit(solution)/shard_map/ppermute | solution.py:287
  347.6 11.2 %collective-permute-start.53 = (bf16[96,384]{1,0:T(8,128)(2,1)S(1)}, bf16[96,384]{1,0:T(8,128)(2,1)S(1)}, u32[]{:S(2)}, u32[]{:S(2)}) collective-permute-start(bf16[96,384]{1,0:T(8,128)(2,1)S(1)} %get-tuple-element.81), channel_id=1, source_target_pairs={{0,8},{4,12},{8,0},{12,4},{16,24},{20,28},{24,16},{28,20},{1,9},{5... | collective-permute-start | bytes 221192 | tf_op jit(solution)/shard_map/ppermute | solution.py:287
  350.1 12.1 %collective-permute-start.44 = (bf16[96,1152]{1,0:T(8,128)(2,1)S(1)}, bf16[96,1152]{1,0:T(8,128)(2,1)S(1)}, u32[]{:S(2)}, u32[]{:S(2)}) collective-permute-start(bf16[96,1152]{1,0:T(8,128)(2,1)S(1)} %get-tuple-element.55), channel_id=1, source_target_pairs={{0,4},{4,0},{8,12},{12,8},{16,20},{20,16},{24,28},{28,24},{1,5},{5... | collective-permute-start | bytes 663560 | tf_op jit(solution)/shard_map/ppermute | solution.py:287
  352.9 11.2 %collective-permute-start.50 = (bf16[96,1152]{1,0:T(8,128)(2,1)S(1)}, bf16[96,1152]{1,0:T(8,128)(2,1)S(1)}, u32[]{:S(2)}, u32[]{:S(2)}) collective-permute-start(bf16[96,1152]{1,0:T(8,128)(2,1)S(1)} %get-tuple-element.56), channel_id=1, source_target_pairs={{0,28},{4,24},{8,20},{12,16},{16,12},{20,8},{24,4},{28,0},{1,29},{... | collective-permute-start | bytes 663560 | tf_op jit(solution)/shard_map/ppermute | solution.py:287
  355.3 25.0 %collective-permute-start.49 = (bf16[96,1152]{1,0:T(8,128)(2,1)S(1)}, bf16[96,1152]{1,0:T(8,128)(2,1)S(1)}, u32[]{:S(2)}, u32[]{:S(2)}) collective-permute-start(bf16[96,1152]{1,0:T(8,128)(2,1)S(1)} %get-tuple-element.57), channel_id=1, source_target_pairs={{0,24},{4,28},{8,16},{12,20},{16,8},{20,12},{24,0},{28,4},{1,25},{... | collective-permute-start | bytes 663560 | tf_op jit(solution)/shard_map/ppermute | solution.py:287
  358.7 30.5 %collective-permute-start.48 = (bf16[96,1152]{1,0:T(8,128)(2,1)S(1)}, bf16[96,1152]{1,0:T(8,128)(2,1)S(1)}, u32[]{:S(2)}, u32[]{:S(2)}) collective-permute-start(bf16[96,1152]{1,0:T(8,128)(2,1)S(1)} %get-tuple-element.58), channel_id=1, source_target_pairs={{0,20},{4,16},{8,28},{12,24},{16,4},{20,0},{24,12},{28,8},{1,21},{... | collective-permute-start | bytes 663560 | tf_op jit(solution)/shard_map/ppermute | solution.py:287
  358.8 33.1 %collective-permute-start.47 = (bf16[96,1152]{1,0:T(8,128)(2,1)S(1)}, bf16[96,1152]{1,0:T(8,128)(2,1)S(1)}, u32[]{:S(2)}, u32[]{:S(2)}) collective-permute-start(bf16[96,1152]{1,0:T(8,128)(2,1)S(1)} %get-tuple-element.59), channel_id=1, source_target_pairs={{0,16},{4,20},{8,24},{12,28},{16,0},{20,4},{24,8},{28,12},{1,17},{... | collective-permute-start | bytes 663560 | tf_op jit(solution)/shard_map/ppermute | solution.py:287
  362.1 31.5 %collective-permute-start.46 = (bf16[96,1152]{1,0:T(8,128)(2,1)S(1)}, bf16[96,1152]{1,0:T(8,128)(2,1)S(1)}, u32[]{:S(2)}, u32[]{:S(2)}) collective-permute-start(bf16[96,1152]{1,0:T(8,128)(2,1)S(1)} %get-tuple-element.60), channel_id=1, source_target_pairs={{0,12},{4,8},{8,4},{12,0},{16,28},{20,24},{24,20},{28,16},{1,13},{... | collective-permute-start | bytes 663560 | tf_op jit(solution)/shard_map/ppermute | solution.py:287
  364.1 29.5 %collective-permute-start.45 = (bf16[96,1152]{1,0:T(8,128)(2,1)S(1)}, bf16[96,1152]{1,0:T(8,128)(2,1)S(1)}, u32[]{:S(2)}, u32[]{:S(2)}) collective-permute-start(bf16[96,1152]{1,0:T(8,128)(2,1)S(1)} %get-tuple-element.61), channel_id=1, source_target_pairs={{0,8},{4,12},{8,0},{12,4},{16,24},{20,28},{24,16},{28,20},{1,9},{5... | collective-permute-start | bytes 663560 | tf_op jit(solution)/shard_map/ppermute | solution.py:287
  380.3 35.1 %collective-permute-start.34 = (bf16[1024,768]{1,0:T(8,128)(2,1)}, bf16[1024,768]{1,0:T(8,128)(2,1)}, u32[]{:S(2)}, u32[]{:S(2)}) collective-permute-start(bf16[1024,768]{1,0:T(8,128)(2,1)} %convolution_convert_fusion.4), channel_id=1, source_target_pairs={{0,1},{1,0},{2,3},{3,2},{4,5},{5,4},{6,7},{7,6},{8,9},{9,8},{10,11... | collective-permute-start | bytes 4718600 | tf_op jit(solution)/shard_map/ppermute | solution.py:301
  389.3 38.6 %collective-permute-start.31 = (bf16[512,768]{1,0:T(8,128)(2,1)}, bf16[512,768]{1,0:T(8,128)(2,1)}, u32[]{:S(2)}, u32[]{:S(2)}) collective-permute-start(bf16[512,768]{1,0:T(8,128)(2,1)} %get-tuple-element.63), channel_id=1, source_target_pairs={{0,2},{2,0},{1,3},{3,1},{4,6},{6,4},{5,7},{7,5},{8,10},{10,8},{9,1... | collective-permute-start | bytes 2359304 | tf_op jit(solution)/shard_map/ppermute | solution.py:481
  391.9 17.5 %collective-permute-start.59 = (bf16[96,384]{1,0:T(8,128)(2,1)S(1)}, bf16[96,384]{1,0:T(8,128)(2,1)S(1)}, u32[]{:S(2)}, u32[]{:S(2)}) collective-permute-start(bf16[96,384]{1,0:T(8,128)(2,1)S(1)} %fusion.54), channel_id=1, source_target_pairs={{0,2},{2,0},{1,3},{3,1},{4,6},{6,4},{5,7},{7,5},{8,10},{10,8},{9,1... | collective-permute-start | bytes 221192 | tf_op jit(solution)/shard_map/ppermute | solution.py:290
  394.8 17.0 %collective-permute-start.51 = (bf16[96,1152]{1,0:T(8,128)(2,1)S(1)}, bf16[96,1152]{1,0:T(8,128)(2,1)S(1)}, u32[]{:S(2)}, u32[]{:S(2)}) collective-permute-start(bf16[96,1152]{1,0:T(8,128)(2,1)S(1)} %fusion.40), channel_id=1, source_target_pairs={{0,2},{2,0},{1,3},{3,1},{4,6},{6,4},{5,7},{7,5},{8,10},{10,8},{9,1... | collective-permute-start | bytes 663560 | tf_op jit(solution)/shard_map/ppermute | solution.py:290
  419.7 11.0 %collective-permute-start.36 = (f32[2,96]{1,0:T(2,128)S(1)}, f32[2,96]{1,0:T(2,128)S(1)}, u32[]{:S(2)}, u32[]{:S(2)}) collective-permute-start(f32[2,96]{1,0:T(2,128)S(1)} %get-tuple-element.84), channel_id=1, source_target_pairs={{0,4},{4,0},{8,12},{12,8},{16,20},{20,16},{24,28},{28,24},{1,5},{5... | collective-permute-start | bytes 2312 | tf_op jit(solution)/shard_map/ppermute | solution.py:287
  421.2 10.7 %collective-permute-start.37 = (f32[2,96]{1,0:T(2,128)S(1)}, f32[2,96]{1,0:T(2,128)S(1)}, u32[]{:S(2)}, u32[]{:S(2)}) collective-permute-start(f32[2,96]{1,0:T(2,128)S(1)} %get-tuple-element.85), channel_id=1, source_target_pairs={{0,8},{4,12},{8,0},{12,4},{16,24},{20,28},{24,16},{28,20},{1,9},{5... | collective-permute-start | bytes 2312 | tf_op jit(solution)/shard_map/ppermute | solution.py:287
  421.2 13.5 %collective-permute-start.38 = (f32[2,96]{1,0:T(2,128)S(1)}, f32[2,96]{1,0:T(2,128)S(1)}, u32[]{:S(2)}, u32[]{:S(2)}) collective-permute-start(f32[2,96]{1,0:T(2,128)S(1)} %get-tuple-element.86), channel_id=1, source_target_pairs={{0,12},{4,8},{8,4},{12,0},{16,28},{20,24},{24,20},{28,16},{1,13},{... | collective-permute-start | bytes 2312 | tf_op jit(solution)/shard_map/ppermute | solution.py:287
  423.3 15.5 %collective-permute-start.39 = (f32[2,96]{1,0:T(2,128)S(1)}, f32[2,96]{1,0:T(2,128)S(1)}, u32[]{:S(2)}, u32[]{:S(2)}) collective-permute-start(f32[2,96]{1,0:T(2,128)S(1)} %get-tuple-element.87), channel_id=1, source_target_pairs={{0,16},{4,20},{8,24},{12,28},{16,0},{20,4},{24,8},{28,12},{1,17},{... | collective-permute-start | bytes 2312 | tf_op jit(solution)/shard_map/ppermute | solution.py:287
  427.9 10.9 %collective-permute-start.40 = (f32[2,96]{1,0:T(2,128)S(1)}, f32[2,96]{1,0:T(2,128)S(1)}, u32[]{:S(2)}, u32[]{:S(2)}) collective-permute-start(f32[2,96]{1,0:T(2,128)S(1)} %get-tuple-element.88), channel_id=1, source_target_pairs={{0,20},{4,16},{8,28},{12,24},{16,4},{20,0},{24,12},{28,8},{1,21},{... | collective-permute-start | bytes 2312 | tf_op jit(solution)/shard_map/ppermute | solution.py:287
  430.8 8.1 %collective-permute-start.41 = (f32[2,96]{1,0:T(2,128)S(1)}, f32[2,96]{1,0:T(2,128)S(1)}, u32[]{:S(2)}, u32[]{:S(2)}) collective-permute-start(f32[2,96]{1,0:T(2,128)S(1)} %get-tuple-element.89), channel_id=1, source_target_pairs={{0,24},{4,28},{8,16},{12,20},{16,8},{20,12},{24,0},{28,4},{1,25},{... | collective-permute-start | bytes 2312 | tf_op jit(solution)/shard_map/ppermute | solution.py:287
  434.7 14.1 %collective-permute-start.35 = (bf16[512,768]{1,0:T(8,128)(2,1)S(1)}, bf16[512,768]{1,0:T(8,128)(2,1)S(1)}, u32[]{:S(2)}, u32[]{:S(2)}) collective-permute-start(bf16[512,768]{1,0:T(8,128)(2,1)S(1)} %slice.120), channel_id=1, source_target_pairs={{0,2},{2,0},{1,3},{3,1},{4,6},{6,4},{5,7},{7,5},{8,10},{10,8},{9,1... | collective-permute-start | bytes 2359304 | tf_op jit(solution)/shard_map/ppermute | solution.py:504
  438.9 9.4 %collective-permute-start.43 = (f32[2,96]{1,0:T(2,128)S(1)}, f32[2,96]{1,0:T(2,128)S(1)}, u32[]{:S(2)}, u32[]{:S(2)}) collective-permute-start(f32[2,96]{1,0:T(2,128)S(1)} %fusion.70), channel_id=1, source_target_pairs={{0,2},{2,0},{1,3},{3,1},{4,6},{6,4},{5,7},{7,5},{8,10},{10,8},{9,1... | collective-permute-start | bytes 2312 | tf_op jit(solution)/shard_map/ppermute | solution.py:290
  (54 other events, 1327.8 us)

commit v2 on v1

--- a/solution.py
+++ b/solution.py
@@ -265,35 +265,170 @@
 swapped = ((0, 1), (1, 0))
 
 
-def gather_rows(shard, after=None):
-    if after is not None:
-        shard, _ = lax.optimization_barrier((shard, after))
+MESH = pl.DeviceIdType.MESH
+
+
+def greet(with_ctx):
     count = lax.axis_size("fsdp")
     me = lax.axis_index("fsdp")
-    whole = jnp.zeros((count,) + shard.shape, shard.dtype)
-    whole = lax.dynamic_update_index_in_dim(whole, shard, me, 0)
+    barrier = pltpu.get_barrier_semaphore()
     for step in range(1, count):
-        came = lax.ppermute(shard, "fsdp", [(i, i ^ step) for i in range(count)])
-        whole = lax.dynamic_update_index_in_dim(whole, came, me ^ step, 0)
-    return whole.reshape((-1,) + shard.shape[1:])
-
-
-def scatter_blocks(blocks):
+        there = lax.rem(me + step, count)
+        pl.semaphore_signal(barrier, inc=1, device_id={"fsdp": there}, device_id_type=MESH)
+    if with_ctx:
+        there = 1 - lax.axis_index("ctx")
+        pl.semaphore_signal(barrier, inc=1, device_id={"ctx": there}, device_id_type=MESH)
+    pl.semaphore_wait(barrier, count - 1 + int(with_ctx))
+
+
+def gather_copies(src, dst, send, recv, local):
     count = lax.axis_size("fsdp")
     me = lax.axis_index("fsdp")
-    total = lax.dynamic_index_in_dim(blocks, me, 0, keepdims=False).astype(jnp.float32)
+    copies = [pltpu.make_async_copy(src, dst.at[me], local)]
     for step in range(1, count):
-        give = lax.dynamic_index_in_dim(blocks, me ^ step, 0, keepdims=False)
-        came = lax.ppermute(give, "fsdp", [(i, i ^ step) for i in range(count)])
-        total = total + came.astype(jnp.float32)
-    low = total.astype(blocks.dtype)
-    other = lax.ppermute(low, "ctx", swapped)
-    return low.astype(jnp.float32) + other.astype(jnp.float32)
-
-
-def scatter_rows(grad):
+        copies.append(
+            pltpu.make_async_remote_copy(
+                src_ref=src,
+                dst_ref=dst.at[me],
+                send_sem=send.at[step - 1],
+                recv_sem=recv.at[step - 1],
+                device_id={"fsdp": lax.rem(me + step, count)},
+                device_id_type=MESH,
+            )
+        )
+    return copies
+
+
+def scatter_copies(src, slots, send, recv, local):
     count = lax.axis_size("fsdp")
-    return scatter_blocks(grad.astype(jnp.bfloat16).reshape(count, -1, grad.shape[1]))
+    me = lax.axis_index("fsdp")
+    copies = [pltpu.make_async_copy(src.at[me], slots.at[0], local)]
+    for step in range(1, count):
+        there = lax.rem(me + step, count)
+        copies.append(
+            pltpu.make_async_remote_copy(
+                src_ref=src.at[there],
+                dst_ref=slots.at[step],
+                send_sem=send.at[step - 1],
+                recv_sem=recv.at[step - 1],
+                device_id={"fsdp": there},
+                device_id_type=MESH,
+            )
+        )
+    return copies
+
+
+def add_up(slots, low, other, out, send, recv):
+    total = slots[0].astype(jnp.float32)
+    for step in range(1, slots.shape[0]):
+        total += slots[step].astype(jnp.float32)
+    low[...] = total.astype(low.dtype)
+    copy = pltpu.make_async_remote_copy(
+        src_ref=low,
+        dst_ref=other,
+        send_sem=send,
+        recv_sem=recv,
+        device_id={"ctx": 1 - lax.axis_index("ctx")},
+        device_id_type=MESH,
+    )
+    copy.start()
+    return copy
+
+
+def finish_sums(groups, ctx_send, ctx_recv):
+    later = []
+    for n, (slots, low, other, out) in enumerate(groups):
+        later.append(add_up(slots, low, other, out, ctx_send.at[n], ctx_recv.at[n]))
+    for copy, (slots, low, other, out) in zip(later, groups):
+        copy.wait()
+        out[...] = low[...].astype(jnp.float32) + other[...].astype(jnp.float32)
+
+
+def semaphores(arrays, count):
+    return [
+        pltpu.SemaphoreType.DMA((arrays, count - 1)),
+        pltpu.SemaphoreType.DMA((arrays, count - 1)),
+        pltpu.SemaphoreType.DMA((arrays,)),
+    ]
+
+
+def gather_kernel(*refs):
+    many = (len(refs) - 3) // 2
+    send, recv, local = refs[-3:]
+    greet(False)
+    copies = []
+    for n in range(many):
+        copies += gather_copies(refs[n], refs[many + n], send.at[n], recv.at[n], local.at[n])
+    for copy in copies:
+        copy.start()
+    for copy in copies:
+        copy.wait()
+
+
+def gather(*shards):
+    count = lax.axis_size("fsdp")
+    return pl.pallas_call(
+        gather_kernel,
+        in_specs=[pl.BlockSpec(memory_space=pl.ANY)] * len(shards),
+        out_specs=[pl.BlockSpec(memory_space=pl.ANY)] * len(shards),
+        out_shape=[jax.ShapeDtypeStruct((count,) + s.shape, s.dtype) for s in shards],
+        scratch_shapes=semaphores(len(shards), count),
+        compiler_params=pltpu.CompilerParams(collective_id=0, has_side_effects=True),
+        name="gather",
+    )(*shards)
+
+
+def sums_scratch(blocks):
+    shapes = []
+    for b in blocks:
+        shapes += [pltpu.VMEM(b.shape, b.dtype)] + [pltpu.VMEM(b.shape[1:], b.dtype)] * 2
+    many = len(blocks)
+    return (
+        shapes
+        + semaphores(many, blocks[0].shape[0])
+        + [pltpu.SemaphoreType.DMA((many,)), pltpu.SemaphoreType.DMA((many,))]
+    )
+
+
+def sums_parts(srcs, outs, scratch):
+    many = len(srcs)
+    send, recv, local, ctx_send, ctx_recv = scratch[3 * many :]
+    copies, groups = [], []
+    for n in range(many):
+        slots, low, other = scratch[3 * n : 3 * n + 3]
+        copies += scatter_copies(srcs[n], slots, send.at[n], recv.at[n], local.at[n])
+        groups.append((slots, low, other, outs[n]))
+    return copies, groups, ctx_send, ctx_recv
+
+
+def scatter_kernel(*refs, many):
+    greet(True)
+    copies, groups, ctx_send, ctx_recv = sums_parts(
+        refs[:many], refs[many : 2 * many], refs[2 * many :]
+    )
+    for copy in copies:
+        copy.start()
+    for copy in copies:
+        copy.wait()
+    finish_sums(groups, ctx_send, ctx_recv)
+
+
+def scatter(*blocks):
+    return pl.pallas_call(
+        partial(scatter_kernel, many=len(blocks)),
+        in_specs=[pl.BlockSpec(memory_space=pl.ANY)] * len(blocks),
+        out_specs=[pl.BlockSpec(memory_space=pltpu.VMEM)] * len(blocks),
+        out_shape=[jax.ShapeDtypeStruct(b.shape[1:], jnp.float32) for b in blocks],
+        scratch_shapes=sums_scratch(blocks),
+        compiler_params=pltpu.CompilerParams(
+            collective_id=1, has_side_effects=True, vmem_limit_bytes=44 << 20
+        ),
+        name="scatter",
+    )(*blocks)
+
+
+def as_blocks(grad):
+    return grad.astype(jnp.bfloat16).reshape(lax.axis_size("fsdp"), -1, grad.shape[1])
 
 
 def sum_tp(part):
@@ -323,7 +458,22 @@
     return jnp.where(lane % HD < HD // 2, -pltpu.roll(u, 96, 1), pltpu.roll(u, 32, 1))
 
 
-def attend_kernel(h_ref, w_ref, cos_ref, sin_ref, q_ref, k_ref, v_ref, o_ref, lse_ref, *, tile):
+def attend_kernel(*refs, tile):
+    h_ref, w_ref, cos_ref, sin_ref = refs[:4]
+    shards = refs[4:7]
+    q_ref, k_ref, v_ref, o_ref, lse_ref = refs[7:12]
+    wholes = refs[12:15]
+    send, recv, local = refs[15:]
+    copies = []
+    for n in range(3):
+        copies += gather_copies(shards[n], wholes[n], send.at[n], recv.at[n], local.at[n])
+
+    @pl.when(pl.program_id(0) == 0)
+    def _():
+        greet(False)
+        for copy in copies:
+            copy.start()
+
     rows = h_ref.shape[0]
     raw = jnp.dot(h_ref[...], w_ref[...], preferred_element_type=jnp.float32)
     cosine, sine = cos_ref[...], sin_ref[...]
@@ -351,10 +501,24 @@
             outs.append(dot(vh, e.astype(jnp.bfloat16), ((1,), (0,))) / total)
         o_ref[at, :] = jnp.concatenate(outs, axis=0).T.astype(jnp.bfloat16)
 
-
-def attend_back_kernel(
-    q_ref, k_ref, v_ref, o_ref, do_ref, lse_ref, cos_ref, sin_ref, out_ref, dk_ref, dv_ref, *, tile
-):
+    @pl.when(pl.program_id(0) == pl.num_programs(0) - 1)
+    def _():
+        for copy in copies:
+            copy.wait()
+
+
+def attend_back_kernel(*refs, tile):
+    q_ref, k_ref, v_ref, o_ref, do_ref, lse_ref, cos_ref, sin_ref = refs[:8]
+    out_ref = refs[11]
+    dk_ref, dv_ref = refs[15:17]
+    copies, groups, ctx_send, ctx_recv = sums_parts(refs[8:11], refs[12:15], refs[17:])
+
+    @pl.when(pl.program_id(0) == 0)
+    def _():
+        greet(True)
+        for copy in copies:
+            copy.start()
+
     rows = q_ref.shape[0]
     k, v = k_ref[...], v_ref[...]
     k_turned = k.astype(jnp.float32).T.astype(jnp.bfloat16)
@@ -384,8 +548,16 @@
     out_ref[:, 128:256] = (dk * cos_ref[...] - turn(dk) * sin_ref[...]).astype(jnp.bfloat16)
     out_ref[:, 256:] = dv_ref[...].astype(jnp.bfloat16)
 
-
-def attend(h_one, w_pairs, cosine, sine):
+    @pl.when(pl.program_id(0) == pl.num_programs(0) - 1)
+    def _():
+        for copy in copies:
+            copy.wait()
+        finish_sums(groups, ctx_send, ctx_recv)
+
+
+def attend(h_one, w_pairs, cosine, sine, *shards):
+    count = lax.axis_size("fsdp")
+    anywhere = [pl.BlockSpec(memory_space=pl.ANY)] * len(shards)
     rows, model = h_one.shape
     pairs = w_pairs.shape[1] // 384
     width = pairs * 128
@@ -400,18 +572,24 @@
             pl.BlockSpec((model, 384), lambda i: (0, i)),
             table,
             table,
-        ],
-        out_specs=[column] * 4 + [pl.BlockSpec((1, 2, rows), lambda i: (i, 0, 0))],
-        out_shape=[low] * 4 + [jax.ShapeDtypeStruct((pairs, 2, rows), jnp.float32)],
-        compiler_params=pltpu.CompilerParams(vmem_limit_bytes=44 << 20),
+        ]
+        + anywhere,
+        out_specs=[column] * 4 + [pl.BlockSpec((1, 2, rows), lambda i: (i, 0, 0))] + anywhere,
+        out_shape=[low] * 4
+        + [jax.ShapeDtypeStruct((pairs, 2, rows), jnp.float32)]
+        + [jax.ShapeDtypeStruct((count,) + s.shape, s.dtype) for s in shards],
+        scratch_shapes=semaphores(len(shards), count),
+        compiler_params=pltpu.CompilerParams(
+            collective_id=2, has_side_effects=True, vmem_limit_bytes=44 << 20
+        ),
         cost_estimate=pl.CostEstimate(
             flops=16 * 10**9, bytes_accessed=10**7, transcendentals=pairs * 2 * rows * rows
         ),
         name="attend",
-    )(h_one, w_pairs, cosine, sine)
-
-
-def attend_back(q, k, v, o, do, lse, cosine, sine):
+    )(h_one, w_pairs, cosine, sine, *shards)
+
+
+def attend_back(q, k, v, o, do, lse, cosine, sine, *blocks):
     rows, width = q.shape
     pairs = width // 128
     column = pl.BlockSpec((rows, 128), lambda i: (0, i))
@@ -419,16 +597,22 @@
     return pl.pallas_call(
         partial(attend_back_kernel, tile=min(512, rows)),
         grid=(pairs,),
-        in_specs=[column] * 5 + [pl.BlockSpec((1, 2, rows), lambda i: (i, 0, 0)), table, table],
-        out_specs=pl.BlockSpec((rows, 384), lambda i: (0, i)),
-        out_shape=jax.ShapeDtypeStruct((rows, 3 * width), jnp.bfloat16),
-        scratch_shapes=[pltpu.VMEM((rows, 128), jnp.float32)] * 2,
-        compiler_params=pltpu.CompilerParams(vmem_limit_bytes=44 << 20),
+        in_specs=[column] * 5
+        + [pl.BlockSpec((1, 2, rows), lambda i: (i, 0, 0)), table, table]
+        + [pl.BlockSpec(memory_space=pl.ANY)] * len(blocks),
+        out_specs=[pl.BlockSpec((rows, 384), lambda i: (0, i))]
+        + [pl.BlockSpec(b.shape[1:], lambda i: (0, 0)) for b in blocks],
+        out_shape=[jax.ShapeDtypeStruct((rows, 3 * width), jnp.bfloat16)]
+        + [jax.ShapeDtypeStruct(b.shape[1:], jnp.float32) for b in blocks],
+        scratch_shapes=[pltpu.VMEM((rows, 128), jnp.float32)] * 2 + sums_scratch(blocks),
+        compiler_params=pltpu.CompilerParams(
+            collective_id=3, has_side_effects=True, vmem_limit_bytes=48 << 20
+        ),
         cost_estimate=pl.CostEstimate(
             flops=30 * 10**9, bytes_accessed=10**7, transcendentals=pairs * 2 * rows * rows
         ),
         name="attend_back",
-    )(q, k, v, o, do, lse, cosine, sine)
+    )(q, k, v, o, do, lse, cosine, sine, *blocks)
 
 
 def rope_tables(rows):
@@ -455,13 +639,13 @@
     packed = jnp.stack(
         [w.reshape(part, pairs, 128) for w in (w_query, w_key, w_value)], axis=2
     ).reshape(part, 3 * width)
-    gains = lax.all_gather(jnp.stack([gain_attn, gain_ffn]), "fsdp", axis=1, tiled=True)
-    gain_one, gain_two = gains[0].astype(jnp.float32), gains[1].astype(jnp.float32)
+    gains = jnp.pad(
+        jnp.stack([gain_attn, gain_ffn]).astype(jnp.float32), ((0, 6), (0, 128 - part))
+    )
     x = take_sequence(tokens).astype(jnp.float32)
-    qkv_w = gather_rows(packed)
-    out_w = gather_rows(w_out.T, qkv_w)
-    ffn_w = gather_rows(jnp.concatenate([w_gate, w_up], axis=1), qkv_w)
-    down_w = gather_rows(w_down.T, qkv_w)
+    qkv_w, gains = gather(packed, gains)
+    qkv_w = qkv_w.reshape(model, -1)
+    gain_one, gain_two = gains[:, 0, :part].reshape(-1), gains[:, 1, :part].reshape(-1)
     cotangent, _ = lax.optimization_barrier((cotangent, qkv_w))
     grad_low = take_sequence(cotangent)
     grad_y = grad_low.astype(jnp.float32)
@@ -469,7 +653,9 @@
 
     normed_one, rstd_one = layer_norm(x)
     h_one = (normed_one * gain_one).astype(jnp.bfloat16)
-    q, k, v, attended, lse = attend(h_one, qkv_w, cosine, sine)
+    shards = (w_out.T, jnp.concatenate([w_gate, w_up], axis=1), w_down.T)
+    q, k, v, attended, lse, *rest = attend(h_one, qkv_w, cosine, sine, *shards)
+    out_w, ffn_w, down_w = (w.reshape(model, -1) for w in rest)
     x_two = x + sum_tp(dot(attended, out_w, ((1,), (1,))))
     normed_two, rstd_two = layer_norm(x_two)
     h_two = (normed_two * gain_two).astype(jnp.bfloat16)
@@ -489,23 +675,28 @@
         axis=1,
     )
     grad_h_two = sum_tp(dot(grad_both, ffn_w, ((1,), (1,))))
-    own_ffn = scatter_rows(dot(h_two, grad_both, ((0,), (0,))))
-    own_down = scatter_rows(dot(grad_low, hidden, ((0,), (0,))))
+    ffn_blocks = as_blocks(dot(h_two, grad_both, ((0,), (0,))))
+    down_blocks = as_blocks(dot(grad_low, hidden, ((0,), (0,))))
     grad_gain_ffn = jnp.sum(grad_h_two * normed_two, axis=0)
     grad_x_two = grad_y + norm_back(grad_h_two * gain_two, normed_two, rstd_two)
     branch_low = grad_x_two.astype(jnp.bfloat16)
-    own_out = scatter_rows(dot(branch_low, attended, ((0,), (0,))))
+    out_blocks = as_blocks(dot(branch_low, attended, ((0,), (0,))))
     grad_att = matmul(branch_low, out_w).astype(jnp.bfloat16)
-    grad_qkv = attend_back(q, k, v, attended, grad_att, lse, cosine, sine)
+    grad_qkv, own_ffn, own_down, own_out = attend_back(
+        q, k, v, attended, grad_att, lse, cosine, sine, ffn_blocks, down_blocks, out_blocks
+    )
     grad_h_one = sum_tp(dot(grad_qkv, qkv_w, ((1,), (1,))))
-    own_qkv = scatter_rows(dot(h_one, grad_qkv, ((0,), (0,))))
+    qkv_blocks = as_blocks(dot(h_one, grad_qkv, ((0,), (0,))))
     grad_gain_attn = jnp.sum(grad_h_one * normed_one, axis=0)
     grad_x = grad_x_two + norm_back(grad_h_one * gain_one, normed_one, rstd_one)
     came = lax.ppermute(grad_x[rows:].astype(jnp.bfloat16), "ctx", swapped).astype(jnp.float32)
     grad_tokens = give_back(grad_x[:rows], came)
-    own_gains = scatter_blocks(
-        jnp.stack([grad_gain_attn, grad_gain_ffn]).reshape(2, -1, part).transpose(1, 0, 2)
-    )
+    gain_blocks = jnp.pad(
+        jnp.stack([grad_gain_attn, grad_gain_ffn]).reshape(2, -1, part).transpose(1, 0, 2),
+        ((0, 0), (0, 6), (0, 128 - part)),
+    )
+    own_qkv, own_gains = scatter(qkv_blocks, gain_blocks)
+    own_gains = own_gains[:, :part]
     own_qkv = own_qkv.reshape(part, pairs, 3, 128)
     return (
         output,

time: 460 us -> 387 us (0.84); the launches traced: 451 us -> 384 us
  Pallas kernels: 34.1 us -> 259 us
  starting transfers between devices: 154 us -> 7.12 us
  waiting for transfers between devices: 141 us -> 25.1 us
  blocking collectives: 28.8 us -> 0 us
  matrix products: 28.4 us -> 39.9 us
  other arithmetic: 38.7 us -> 29.4 us
    ppermute x68 -> x0, starting transfers between devices: 149 us -> none  [the longest x35 88 us: scatter_blocks(): came = lax.ppermute(give, 'fsdp', [(i, i ^ step) for i in range(count)])]
    ppermute x68 -> x0, waiting for transfers between devices: 138 us -> none  [the longest x28 75.2 us: gather_rows(): came = lax.ppermute(shard, 'fsdp', [(i, i ^ step) for i in range(count)])]
    pallas_call x0 -> x2, Pallas kernels: none -> 98.3 us  [the longest x1 53.9 us: scatter(): pl.pallas_call(partial(scatter_kernel, many=len(blocks)), in_specs=[pl.Bl...]
    pallas_call x1, Pallas kernels: 17.8 us -> 89.8 us  [attend_back(): pl.pallas_call(partial(attend_back_kernel, tile=min(512, rows)), grid=(pa...]
    pallas_call x1, Pallas kernels: 16.3 us -> 71.1 us  [attend(): pl.pallas_call(partial(attend_kernel, tile=min(512, rows)), grid=(pairs,)...]
    all_gather x1 -> x0, blocking collectives: 28.8 us -> none  [on_device(): lax.all_gather(jnp.stack([gain_attn, gain_ffn]), 'fsdp', axis=1, tiled=True)]
    ppermute x1, waiting for transfers between devices: 0.01 us -> 13.9 us  [on_device(): lax.ppermute(output[rows:], 'ctx', swapped)]
    convert_element_type x1, other arithmetic: 12.5 us -> 0.86 us  [on_device(): (grad_hidden * activated).astype(jnp.bfloat16)]
  transfers between devices with their start and end apart: 76 -> 8, of which waited for: 27 -> 3; matrix products, arithmetic and copies ran while one was open for 9% -> 11% of each run, Pallas kernels for 4% -> 26%
where the time goes in v2:
time: 387 us; the launch traced here: 384 us
  Pallas kernels  259 us (67%)
  matrix products  39.9 us (10%)
  other arithmetic  29.4 us (8%)
  waiting for transfers between devices  25.1 us (6%)
  local copies, waits for them, and re-layouts  21.3 us (6%)
  starting transfers between devices  7.12 us (2%)
    pallas_call x1, Pallas kernels, attend_back(): pl.pallas_call(partial(attend_back_kernel, tile=min(512, rows)), grid=(pa...  89.8 us
    pallas_call x1, Pallas kernels, attend(): pl.pallas_call(partial(attend_kernel, tile=min(512, rows)), grid=(pairs,)...  71.1 us
    pallas_call x1, Pallas kernels, scatter(): pl.pallas_call(partial(scatter_kernel, many=len(blocks)), in_specs=[pl.Bl...  53.9 us
    pallas_call x1, Pallas kernels, gather(): pl.pallas_call(gather_kernel, in_specs=[pl.BlockSpec(memory_space=pl.ANY)...  44.4 us
    dot_general x8, matrix products, dot(): lax.dot_general(a, b, (over, ((), ())), preferred_element_type=jnp.float32)  27.9 us
    ppermute x1, waiting for transfers between devices, on_device(): lax.ppermute(output[rows:], 'ctx', swapped)  13.9 us
    dot_general x3, matrix products, matmul(): return jnp.dot(a, b, preferred_element_type=jnp.float32)  12.1 us
    ppermute x2, waiting for transfers between devices, take_sequence(): return jnp.concatenate([own, lax.ppermute(give, 'ctx', swapped)], axis=0)  9.81 us
  transfers between devices with their start and end apart: 8, of which 3 were waited for; matrix products, arithmetic and copies ran while one was open for 11% of the time, Pallas kernels for 26%

profile of v2, /device:TPU:0, one launch (start us, length us, event | category | flops | bytes accessed | tf_op | source)
XLA Modules:
  0.0 383.6 jit_solution(2403714779942228178)
XLA Ops:
  0.7 1.6 dynamic-slice_bitcast_fusion.3
  2.3 3.0 collective-permute-start
  5.4 0.2 pad_maximum_fusion.7
  5.7 0.3 copy.33
  6.0 0.9 reshape.99.refs_0_
  6.9 0.6 fusion.33.refs_1_
  7.5 44.4 %gather.1 = (bf16[8,96,1152]{2,1,0:T(8,128)(2,1)}, f32[8,8,128]{2,1,0:T(8,128)}) custom-call(bf16[96,1152]{1,0:T(8,128)(2,1)} %reshape.99.refs_0_, f32[8,128]{1,0:T(8,128)} %fusion.33.refs_1_), custom_call_target="tpu_custom_call" | custom-call | tf_op jit(solution)/shard_map/gather/pallas_call | solution.py:370
  51.9 0.9 slice_reduce_fusion.3
  53.0 1.3 broadcast_select_fusion
  54.3 0.3 convert_reduce_fusion
  54.6 0.6 fusion.12
  55.3 0.5 fusion.6.refs_0_
  55.9 71.1 %attend.1 = (bf16[1024,384]{1,0:T(8,128)(2,1)S(1)}, bf16[1024,384]{1,0:T(8,128)(2,1)S(1)}, bf16[1024,384]{1,0:T(8,128)(2,1)S(1)}, bf16[1024,384]{1,0:T(8,128)(2,...) custom-call(bf16[1024,768]{1,0:T(8,128)(2,1)S(1)} %fusion.6.refs_0_,, ...), custom_call_target="tpu_custom_call" | custom-call | flops 16000000000 | bytes 10000000 | tf_op jit(solution)/shard_map/attend/pallas_call | solution.py:567
  127.0 2.2 convolution_convert_fusion.3
  129.2 0.4 copy-done.29
  129.6 1.3 dynamic-slice_bitcast_fusion.1
  130.9 0.6 collective-permute-start.4
  131.5 1.4 collective-permute-done.1
  132.9 3.0 fusion.40
  136.0 0.5 multiply_reduce_fusion.2
  136.5 2.1 copy-done.9
  138.6 2.4 fusion.38
  141.0 9.8 %collective-permute-done.4 = bf16[512,768]{1,0:T(8,128)(2,1)} collective-permute-done((bf16[512,768]{1,0:T(8,128)(2,1)}, bf16[512,768]{1,0:T(8,128)(2,1)}, u32[]{:S(2)}, u32[]{:S(2)}) %collective-permute-start.4) | collective-permute-done | bytes 786464 | tf_op jit(solution)/shard_map/ppermute | solution.py:444
  150.8 7.8 %add_convert_fusion.1 = (bf16[1024,576]{1,0:T(8,128)(2,1)S(1)}, f32[1024,576]{1,0:T(8,128)S(1)}, f32[1024,576]{1,0:T(8,128)S(1)}) fusion(f32[1024,1152]{1,0:T(8,128)S(1)} %fusion.38, bf16[768,576]{1,0:T(8,128)(2,1)S(1)} %bitcast.72, bf16[512,768]{1,0:T(8,128)(2,1)} %collective-permute-done.4, bf16[512,768]{1,0:T(8,128)(2,1)S(1)} %copy-done.26), kind=kOutput, calls=%fused_computation.33 | convolution fusion | flops 952172544 | bytes 13074432 | tf_op jit(solution)/shard_map/dot_general | solution.py:49
  158.6 0.9 multiply_convert_fusion.1
  159.5 0.2 copy-done.39
  159.7 3.4 convolution_convert_fusion.5
  163.1 2.6 convolution_convert_fusion.2
  165.7 0.5 collective-permute-start.2
  166.2 3.2 convolution_convert_fusion.6
  169.4 2.3 copy.38
  171.6 6.4 %convolution_convert_fusion.1 = bf16[768,1152]{1,0:T(8,128)(2,1)} fusion(bf16[1024,576]{1,0:T(8,128)(2,1)} %copy-done.30, bf16[1024,576]{1,0:T(8,128)(2,1)} %copy-done.39, f32[1024,768]{1,0:T(8,128)} %copy-done.18, f32[768]{0:T(1024)S(1)} %mul.142, f32[1024]{0:T(1024)S(1)} %add_rsqrt_fusion, f32[1024]{0:T(1024)S(1)} %broadcast_multiply_fusion.4), kind=kOutput, calls=%fused_computation.11 | convolution fusion | flops 1820688384 | bytes 7285760 | tf_op jit(solution)/shard_map/dot_general | solution.py:453
  178.1 3.1 multiply_reduce_fusion
  181.3 4.2 %multiply_add_fusion = (f32[1024,768]{1,0:T(8,128)S(1)}, bf16[1024,768]{1,0:T(8,128)(2,1)S(1)}) fusion(bf16[1024,768]{1,0:T(8,128)(2,1)} %collective-permute-done.5, bf16[1024,768]{1,0:T(8,128)(2,1)} %convolution_convert_fusion.5, f32[1024,768]{1,0:T(8,128)S(1)} %copy-done.19, f32[1024]{0:T(1024)S(1)} %broadcast_multiply_fusion.2, ...), kind=kLoop, calls=%fused_computation.22 | loop fusion | flops 15728640 | bytes 15748096 | tf_op jit(solution)/shard_map/add | solution.py:681
  185.5 1.9 convolution_convert_fusion.7.refs_4_
  187.4 1.0 convolution_convert_fusion.8
  188.5 0.1 copy-done.3
  188.6 0.3 copy-done.13
  188.9 0.2 copy-done.15
  189.1 0.2 copy-done.17
  189.4 89.8 %attend_back.1 = (bf16[1024,1152]{1,0:T(8,128)(2,1)}, f32[96,1152]{1,0:T(8,128)S(1)}, f32[96,576]{1,0:T(8,128)S(1)}, f32[96,384]{1,0:T(8,128)S(1)}) custom-call(bf16[1024,384]{1,0:T(8,128)(2,1)S(1)} %copy-done.13, bf16[1024,384]{1,0:T(8,128)(2,1)S(1)} %copy-done.15, bf16[1024,384]{1,0:T(8,128)(2,1)S(1)} %copy-done.17, ...), custom_call_target="tpu_custom_call" | custom-call | flops 30000001024 | bytes 10000000 | tf_op jit(solution)/shard_map/attend_back/pallas_call | solution.py:597
  279.2 5.1 %convolution_convert_fusion.4 = bf16[1024,768]{1,0:T(8,128)(2,1)} fusion(bf16[1024,1152]{1,0:T(8,128)(2,1)} %get-tuple-element.39, bf16[768,1152]{1,0:T(8,128)(2,1)S(1)} %bitcast.84), kind=kOutput, calls=%fused_computation.55 | convolution fusion | flops 1812725760 | bytes 5701632 | tf_op jit(solution)/shard_map/dot_general | solution.py:453
  284.3 1.3 slice_bitcast_fusion.1
  285.6 1.5 collective-permute-start.3
  287.1 0.8 fusion.41
  288.0 4.0 %convolution_convert_fusion = bf16[768,1152]{1,0:T(8,128)(2,1)S(1)} fusion(bf16[1024,768]{1,0:T(8,128)(2,1)S(1)} %fusion.6.refs_0_, bf16[1024,1152]{1,0:T(8,128)(2,1)} %get-tuple-element.39), kind=kOutput, calls=%fused_computation.10 | convolution fusion | flops 1812824064 | bytes 5701632 | tf_op jit(solution)/shard_map/dot_general | solution.py:453
  292.0 13.9 %collective-permute-done.3 = bf16[512,768]{1,0:T(8,128)(2,1)} collective-permute-done((bf16[512,768]{1,0:T(8,128)(2,1)}, bf16[512,768]{1,0:T(8,128)(2,1)}, u32[]{:S(2)}, u32[]{:S(2)}) %collective-permute-start.3) | collective-permute-done | bytes 786464 | tf_op jit(solution)/shard_map/ppermute | solution.py:667
  305.8 2.9 maximum_select_fusion.1
  308.7 3.9 %fusion.11 = (f32[768]{0:T(1024)S(1)}, f32[1024]{0:T(1024)S(1)}, f32[1024]{0:T(1024)S(1)}) fusion(bf16[1024,768]{1,0:T(8,128)(2,1)} %collective-permute-done.6, bf16[1024,768]{1,0:T(8,128)(2,1)} %convolution_convert_fusion.4, f32[1024]{0:T(1024)S(1)} %add_rsqrt_fusion.1, f32[1024]{0:T(1024)S(1)} %broadcast_multiply_fusion.5, ...), kind=kLoop, calls=%fused_computation.17 | loop fusion | flops 11793664 | bytes 4741120 | tf_op jit(solution)/shard_map/reduce_sum | solution.py:690
  312.8 4.0 %fusion.10 = f32[1024,768]{1,0:T(8,128)S(1)} fusion(f32[1024,768]{1,0:T(8,128)} %copy-done.20, bf16[1024,768]{1,0:T(8,128)(2,1)} %collective-permute-done.6, bf16[1024,768]{1,0:T(8,128)(2,1)} %convolution_convert_fusion.4, f32[1024]{0:T(1024)S(1)} %broadcast_multiply_fusion, f32[1024]{0:T(1024)S(1)} %broadcast_multiply_fusion.1, f32[768]{0:T(1024)S(1)} %mul.136, ...), kind=kLoop, calls=%fused_computation.16 | loop fusion | flops 11796480 | bytes 11029504 | tf_op jit(solution)/shard_map/add | solution.py:691
  316.8 1.1 slice.115
  317.9 1.5 collective-permute-start.7
  319.4 53.9 %scatter.1 = (f32[96,1152]{1,0:T(8,128)S(1)}, f32[8,128]{1,0:T(8,128)S(1)}) custom-call(bf16[8,96,1152]{2,1,0:T(8,128)(2,1)S(1)} %bitcast.62, f32[8,8,128]{2,1,0:T(8,128)S(1)} %pad.12.refs_1_), custom_call_target="tpu_custom_call" | custom-call | tf_op jit(solution)/shard_map/scatter/pallas_call | solution.py:417
  373.4 0.2 reshape.108
  373.5 1.3 slice_reduce_fusion
  374.8 0.7 copy.50
  375.5 0.7 copy.51
  376.2 0.7 copy.52
  376.9 0.5 slice_bitcast_fusion.2
  377.4 1.5 slice_bitcast_fusion
  378.9 1.2 bitcast_convert_fusion
  380.1 1.9 maximum_select_fusion
  382.0 0.7 copy.55
  382.7 0.7 copy.56
  (99 shorter events, 0.7 us)
Async XLA Ops:
  0.6 4.7 %copy-start.33 = (bf16[96,384]{1,0:T(8,128)(2,1)S(1)}, bf16[96,384]{1,0:T(8,128)(2,1)}, u32[]{:S(2)}) copy-start(bf16[96,384]{1,0:T(8,128)(2,1)} %param.15) | copy-start | bytes 221188
  0.7 4.7 %copy-start.34 = (bf16[96,384]{1,0:T(8,128)(2,1)S(1)}, bf16[96,384]{1,0:T(8,128)(2,1)}, u32[]{:S(2)}) copy-start(bf16[96,384]{1,0:T(8,128)(2,1)} %param.16) | copy-start | bytes 221188
  0.7 4.7 %copy-start.35 = (bf16[96,384]{1,0:T(8,128)(2,1)S(1)}, bf16[96,384]{1,0:T(8,128)(2,1)}, u32[]{:S(2)}) copy-start(bf16[96,384]{1,0:T(8,128)(2,1)} %param.17) | copy-start | bytes 221188
  0.7 6.2 %copy-start.36 = (bf16[96]{0:T(256)(128)(2,1)S(1)}, bf16[96]{0:T(256)(128)(2,1)}, u32[]{:S(2)}) copy-start(bf16[96]{0:T(256)(128)(2,1)} %param.19) | copy-start | bytes 580
  0.7 6.2 %copy-start.37 = (bf16[96]{0:T(256)(128)(2,1)S(1)}, bf16[96]{0:T(256)(128)(2,1)}, u32[]{:S(2)}) copy-start(bf16[96]{0:T(256)(128)(2,1)} %param.14) | copy-start | bytes 580
  0.7 52.2 %copy-start.31 = (bf16[96,576]{1,0:T(8,128)(2,1)S(1)}, bf16[96,576]{1,0:T(8,128)(2,1)}, u32[]{:S(2)}) copy-start(bf16[96,576]{1,0:T(8,128)(2,1)} %param.21) | copy-start | bytes 331780
  0.7 52.2 %copy-start.32 = (bf16[96,576]{1,0:T(8,128)(2,1)S(1)}, bf16[96,576]{1,0:T(8,128)(2,1)}, u32[]{:S(2)}) copy-start(bf16[96,576]{1,0:T(8,128)(2,1)} %param.20) | copy-start | bytes 331780
  2.3 52.9 %copy-start.21 = (bf16[512,768]{1,0:T(8,128)(2,1)}, bf16[512,768]{1,0:T(8,128)(2,1)S(1)}, u32[]{:S(2)}) copy-start(bf16[512,768]{1,0:T(8,128)(2,1)S(1)} %get-tuple-element.68) | copy-start | bytes 2359300
  2.3 52.0 %collective-permute-start = (bf16[512,768]{1,0:T(8,128)(2,1)S(1)}, bf16[512,768]{1,0:T(8,128)(2,1)S(1)}, u32[]{:S(2)}, u32[]{:S(2)}) collective-permute-start(bf16[512,768]{1,0:T(8,128)(2,1)S(1)} %get-tuple-element.69), channel_id=1, source_target_pairs={{0,2},{2,0},{1,3},{3,1},{4,6},{6,4},{5,7},{7,5},{8,10},{10,8},{9,1... | collective-permute-start | bytes 2359304 | tf_op jit(solution)/shard_map/ppermute | solution.py:444
  54.3 1.5 copy-start
  54.3 1.5 copy-start.2
  54.3 1.5 copy-start.23
  54.6 1.2 copy-start.6
  54.6 1.2 copy-start.7
  127.0 3.9 %copy-start.8 = (bf16[8,96,1152]{2,1,0:T(8,128)(2,1)}, bf16[8,96,1152]{2,1,0:T(8,128)(2,1)S(1)}, u32[]{:S(2)}) copy-start(bf16[8,96,1152]{2,1,0:T(8,128)(2,1)S(1)} %get-tuple-element.32) | copy-start | bytes 5308420
  127.0 3.9 %copy-start.10 = (bf16[8,96,576]{2,1,0:T(8,128)(2,1)}, bf16[8,96,576]{2,1,0:T(8,128)(2,1)S(1)}, u32[]{:S(2)}) copy-start(bf16[8,96,576]{2,1,0:T(8,128)(2,1)S(1)} %get-tuple-element.33) | copy-start | bytes 2654212
  127.0 3.9 %copy-start.12 = (bf16[1024,384]{1,0:T(8,128)(2,1)}, bf16[1024,384]{1,0:T(8,128)(2,1)S(1)}, u32[]{:S(2)}) copy-start(bf16[1024,384]{1,0:T(8,128)(2,1)S(1)} %get-tuple-element.35.refs_0_) | copy-start | bytes 2359300
  127.0 3.9 %copy-start.14 = (bf16[1024,384]{1,0:T(8,128)(2,1)}, bf16[1024,384]{1,0:T(8,128)(2,1)S(1)}, u32[]{:S(2)}) copy-start(bf16[1024,384]{1,0:T(8,128)(2,1)S(1)} %get-tuple-element.36.refs_1_) | copy-start | bytes 2359300
  127.0 3.9 %copy-start.16 = (bf16[1024,384]{1,0:T(8,128)(2,1)}, bf16[1024,384]{1,0:T(8,128)(2,1)S(1)}, u32[]{:S(2)}) copy-start(bf16[1024,384]{1,0:T(8,128)(2,1)S(1)} %get-tuple-element.37.refs_2_) | copy-start | bytes 2359300
  127.0 2.6 copy-start.29
  129.2 3.8 collective-permute-start.1
  130.9 19.9 %collective-permute-start.4 = (bf16[512,768]{1,0:T(8,128)(2,1)}, bf16[512,768]{1,0:T(8,128)(2,1)}, u32[]{:S(2)}, u32[]{:S(2)}) collective-permute-start(bf16[512,768]{1,0:T(8,128)(2,1)} %get-tuple-element.67), channel_id=1, source_target_pairs={{0,2},{2,0},{1,3},{3,1},{4,6},{6,4},{5,7},{7,5},{8,10},{10,8},{9,1... | collective-permute-start | bytes 2359304 | tf_op jit(solution)/shard_map/ppermute | solution.py:444
  135.9 5.1 %copy-start.18 = (f32[1024,768]{1,0:T(8,128)}, f32[1024,768]{1,0:T(8,128)S(1)}, u32[]{:S(2)}) copy-start(f32[1024,768]{1,0:T(8,128)S(1)} %get-tuple-element.59) | copy-start | bytes 9437188
  136.0 2.6 copy-start.9
  138.6 12.3 %copy-start.11 = (bf16[8,96,576]{2,1,0:T(8,128)(2,1)S(1)}, bf16[8,96,576]{2,1,0:T(8,128)(2,1)}, u32[]{:S(2)}) copy-start(bf16[8,96,576]{2,1,0:T(8,128)(2,1)} %copy-done.10) | copy-start | bytes 2654212
  138.6 12.3 %copy-start.26 = (bf16[512,768]{1,0:T(8,128)(2,1)S(1)}, bf16[512,768]{1,0:T(8,128)(2,1)}, u32[]{:S(2)}) copy-start(bf16[512,768]{1,0:T(8,128)(2,1)} %get-tuple-element.66) | copy-start | bytes 2359300
  158.6 1.1 copy-start.39
  159.5 3.6 copy-start.30
  163.1 15.0 %collective-permute-start.5 = (bf16[1024,768]{1,0:T(8,128)(2,1)}, bf16[1024,768]{1,0:T(8,128)(2,1)}, u32[]{:S(2)}, u32[]{:S(2)}) collective-permute-start(bf16[1024,768]{1,0:T(8,128)(2,1)} %convolution_convert_fusion.5), channel_id=1, source_target_pairs={{0,1},{1,0},{2,3},{3,2},{4,5},{5,4},{6,7},{7,6},{8,9},{9,8},{10,11... | collective-permute-start | bytes 4718600 | tf_op jit(solution)/shard_map/ppermute | solution.py:436
  165.7 15.6 %collective-permute-start.2 = (bf16[1024,768]{1,0:T(8,128)(2,1)}, bf16[1024,768]{1,0:T(8,128)(2,1)}, u32[]{:S(2)}, u32[]{:S(2)}) collective-permute-start(bf16[1024,768]{1,0:T(8,128)(2,1)} %convolution_convert_fusion.2), channel_id=1, source_target_pairs={{0,1},{1,0},{2,3},{3,2},{4,5},{5,4},{6,7},{7,6},{8,9},{9,8},{10,11... | collective-permute-start | bytes 4718600 | tf_op jit(solution)/shard_map/ppermute | solution.py:436
  171.6 6.4 %copy-start.19 = (f32[1024,768]{1,0:T(8,128)S(1)}, f32[1024,768]{1,0:T(8,128)}, u32[]{:S(2)}) copy-start(f32[1024,768]{1,0:T(8,128)} %copy-done.18) | copy-start | bytes 9437188
  178.1 3.2 copy-start.27
  185.5 3.0 copy-start.20
  187.4 1.0 copy-start.1
  187.4 1.2 copy-start.3
  187.4 1.4 copy-start.13
  187.4 1.7 copy-start.15
  187.4 1.9 copy-start.17
  189.3 89.8 %copy-start.38 = (bf16[8,96,1152]{2,1,0:T(8,128)(2,1)S(1)}, bf16[8,96,1152]{2,1,0:T(8,128)(2,1)}, u32[]{:S(2)}) copy-start(bf16[8,96,1152]{2,1,0:T(8,128)(2,1)} %get-tuple-element.29) | copy-start | bytes 5308420
  279.2 5.1 %copy-start.4 = (f32[96,576]{1,0:T(8,128)}, f32[96,576]{1,0:T(8,128)S(1)}, u32[]{:S(2)}) copy-start(f32[96,576]{1,0:T(8,128)S(1)} %get-tuple-element.44) | copy-start | bytes 663556
  284.3 24.4 %collective-permute-start.6 = (bf16[1024,768]{1,0:T(8,128)(2,1)}, bf16[1024,768]{1,0:T(8,128)(2,1)}, u32[]{:S(2)}, u32[]{:S(2)}) collective-permute-start(bf16[1024,768]{1,0:T(8,128)(2,1)} %convolution_convert_fusion.4), channel_id=1, source_target_pairs={{0,1},{1,0},{2,3},{3,2},{4,5},{5,4},{6,7},{7,6},{8,9},{9,8},{10,11... | collective-permute-start | bytes 4718600 | tf_op jit(solution)/shard_map/ppermute | solution.py:436
  285.6 20.3 %collective-permute-start.3 = (bf16[512,768]{1,0:T(8,128)(2,1)}, bf16[512,768]{1,0:T(8,128)(2,1)}, u32[]{:S(2)}, u32[]{:S(2)}) collective-permute-start(bf16[512,768]{1,0:T(8,128)(2,1)} %get-tuple-element.65), channel_id=1, source_target_pairs={{0,2},{2,0},{1,3},{3,1},{4,6},{6,4},{5,7},{7,5},{8,10},{10,8},{9,1... | collective-permute-start | bytes 2359304 | tf_op jit(solution)/shard_map/ppermute | solution.py:667
  288.0 17.9 %copy-start.28 = (bf16[1,512,768]{2,1,0:T(8,128)(2,1)S(1)}, bf16[1,512,768]{2,1,0:T(8,128)(2,1)}, u32[]{:S(2)}) copy-start(bf16[1,512,768]{2,1,0:T(8,128)(2,1)} %get-tuple-element.64) | copy-start | bytes 2359300
  292.0 16.8 %copy-start.22 = (bf16[512,768]{1,0:T(8,128)(2,1)S(1)}, bf16[512,768]{1,0:T(8,128)(2,1)}, u32[]{:S(2)}) copy-start(bf16[512,768]{1,0:T(8,128)(2,1)} %copy-done.21) | copy-start | bytes 2359300
  292.0 16.8 %copy-start.24 = (bf16[512,768]{1,0:T(8,128)(2,1)S(1)}, bf16[512,768]{1,0:T(8,128)(2,1)}, u32[]{:S(2)}) copy-start(bf16[512,768]{1,0:T(8,128)(2,1)} %copy-done.23) | copy-start | bytes 2359300
  316.8 2.6 copy-start.25
  317.9 61.0 %collective-permute-start.7 = (bf16[512,768]{1,0:T(8,128)(2,1)}, bf16[512,768]{1,0:T(8,128)(2,1)}, u32[]{:S(2)}, u32[]{:S(2)}) collective-permute-start(bf16[512,768]{1,0:T(8,128)(2,1)} %slice.115), channel_id=1, source_target_pairs={{0,2},{2,0},{1,3},{3,1},{4,6},{6,4},{5,7},{7,5},{8,10},{10,8},{9,1... | collective-permute-start | bytes 2359304 | tf_op jit(solution)/shard_map/ppermute | solution.py:692
  380.1 2.5 copy-start.5
